TPU v7x, 128 devices: a whole 4x4x4 slice. The times are simulated.
128 devices in a mesh: row: 16 (over y, x), col: 8 (over z, core).
Axes of the slice: x: 4, y: 4, z: 4, core: 2. Of those that a mesh axis runs over, the one named last changes fastest.
Arguments:
- object_field: float32 [2, 8192, 4096], P(None, 'row', 'col'), may hold values from -6 to 6
- probe: float32 [2, 256, 256], replicated, may hold values from -6 to 6
- amplitude: float32 [16, 8, 4, 256, 256], P('row', 'col'), may hold values from 0.1 to 3
- positions: int32 [16, 8, 4, 2], P('row', 'col'), may hold values from 0 to 511
- counts: int32 [16, 8], P('row', 'col'), may hold values from 1 to 4, as said below
Outputs:
- object_out: float32 [2, 8192, 4096], P(None, 'row', 'col')
- probe_out: float32 [2, 256, 256], replicated
Inputs may be any that keep to these rules, and one draw needn't show every extreme that they name: `counts`: every device has 1 to 4 live slots, its first ones; some device has 4 in every draw and about a quarter have 4, the rest at most half of it.
All inputs are finite; a program needn't handle non-finite values.
Results may differ from a plain program's by a relative error of at most 0.0003.
Values sent between devices are 32-bit elements; how exact they have to be, the bound alone decides.
No kernel may reach another device: no remote copies, remote signals or barrier semaphores. Data moves between devices by JAX's collectives and lax.ppermute only.
A program may use at most 128 MiB of HBM per device.

v0:
```python
import math

import jax
import jax.numpy as jnp
from jax import lax
from jax.sharding import PartitionSpec as P

PASSES = 3


amp_floor = 0.1
object_damping = 0.5
probe_damping = 1.0


def passed_along(block, axis, distance):
    devices = range(lax.axis_size(axis))
    route = [((i - distance) % len(devices), i) for i in devices]
    return lax.ppermute(block, axis, route)


def tables(frame_size):
    indices = jnp.arange(frame_size, dtype=jnp.int32)
    product = indices[:, None] * indices[None, :] % frame_size
    angles = product.astype(jnp.float32) * (-2.0 * math.pi / frame_size)
    factor = 1.0 / math.sqrt(frame_size)
    return (jnp.cos(angles) * factor, jnp.sin(angles) * factor)


def transform(real_part, imag_part, table_re, table_im):
    highest = lax.Precision.HIGHEST

    def on_left(matrix, operand):
        return jnp.einsum("jk,pkl->pjl", matrix, operand, precision=highest)

    def on_right(operand, matrix):
        return jnp.einsum("pjk,kl->pjl", operand, matrix, precision=highest)

    left_re = on_left(table_re, real_part) - on_left(table_im, imag_part)
    left_im = on_left(table_re, imag_part) + on_left(table_im, real_part)
    out_re = on_right(left_re, table_re) - on_right(left_im, table_im)
    out_im = on_right(left_re, table_im) + on_right(left_im, table_re)
    return (out_re, out_im)


def slice_patches(source, row_starts, col_starts, frame_size):

    def one_patch(row_at, col_at):
        anchor = jnp.zeros((), jnp.int32)
        return lax.dynamic_slice(
            source, (anchor, row_at, col_at), (source.shape[0], frame_size, frame_size)
        )

    return jax.vmap(one_patch)(row_starts, col_starts)


def deposit(canvas, pieces, row_starts, col_starts):
    frame_size = pieces.shape[-1]

    def add_one(slot_index, running):
        anchor = jnp.zeros((), jnp.int32)
        corner_at = (anchor, row_starts[slot_index], col_starts[slot_index])
        current = lax.dynamic_slice(running, corner_at, (running.shape[0], frame_size, frame_size))
        return lax.dynamic_update_slice(running, current + pieces[slot_index], corner_at)

    return lax.fori_loop(0, pieces.shape[0], add_one, canvas)


def shards(object_field, probe, amplitude, positions, counts):
    tile_size = object_field.shape[1]
    frame_size = probe.shape[1]
    slot_count = positions.shape[2]
    own_rows = positions[0, 0, :, 0]
    own_cols = positions[0, 0, :, 1]
    active = (jnp.arange(slot_count, dtype=jnp.int32) < counts[0, 0]).astype(jnp.float32)
    measured = amplitude[0, 0]
    table_re, table_im = tables(frame_size)
    estimate = object_field
    probe_now = probe
    for sweep_index in range(PASSES):
        right_strip = passed_along(estimate[:, :, :frame_size], "col", -1)
        widened = jnp.concatenate([estimate, right_strip], axis=2)
        lower_strip = passed_along(widened[:, :frame_size, :], "row", -1)
        extended = jnp.concatenate([widened, lower_strip], axis=1)
        patches = slice_patches(extended, own_rows, own_cols, frame_size)
        patch_re = patches[:, 0]
        patch_im = patches[:, 1]
        probe_re = probe_now[0]
        probe_im = probe_now[1]
        wave_re = probe_re * patch_re - probe_im * patch_im
        wave_im = probe_re * patch_im + probe_im * patch_re
        far_re, far_im = transform(wave_re, wave_im, table_re, table_im)
        modulus = jnp.sqrt(far_re * far_re + far_im * far_im)
        ratio = measured / jnp.maximum(modulus, amp_floor) - 1.0
        back_re, back_im = transform(far_re * ratio, far_im * ratio, table_re, -table_im)
        weight = active[:, None, None]
        back_re = back_re * weight
        back_im = back_im * weight
        update_re = probe_re * back_re + probe_im * back_im
        update_im = probe_re * back_im - probe_im * back_re
        glow = probe_re * probe_re + probe_im * probe_im
        pieces = jnp.stack([update_re, update_im, glow[None] * weight], axis=1)
        canvas = jnp.zeros(
            (pieces.shape[1], tile_size + frame_size, tile_size + frame_size), jnp.float32
        )
        canvas = deposit(canvas, pieces, own_rows, own_cols)
        from_left = passed_along(canvas[:, :, tile_size:], "col", 1)
        canvas = canvas.at[:, :, :frame_size].add(from_left)
        from_above = passed_along(canvas[:, tile_size:, :tile_size], "row", 1)
        summed = canvas[:, :tile_size, :tile_size].at[:, :frame_size, :].add(from_above)
        lighting = summed[2]
        grad_re = jnp.sum(patch_re * back_re + patch_im * back_im, axis=0)
        grad_im = jnp.sum(patch_re * back_im - patch_im * back_re, axis=0)
        power_sum = jnp.sum((patch_re * patch_re + patch_im * patch_im) * weight, axis=0)
        grad_re, grad_im, power_sum = lax.psum((grad_re, grad_im, power_sum), ("row", "col"))
        estimate = estimate + summed[:2] / (lighting + object_damping)
        probe_now = probe_now + jnp.stack([grad_re, grad_im]) / (power_sum + probe_damping)
    return (estimate, probe_now)


def solution(mesh):
    return jax.shard_map(
        shards,
        mesh=mesh,
        in_specs=(
            P(None, "row", "col"),
            P(),
            P("row", "col", None, None, None),
            P("row", "col", None, None),
            P("row", "col"),
        ),
        out_specs=(P(None, "row", "col"), P()),
        check_vma=False,
    )
```

profile of v0, /device:TPU:1, one launch (start us, length us, event | category | flops | bytes accessed | tf_op | source)
XLA Modules:
  0.0 1202.1 jit_solution(6610393475691331594)
XLA Ops:
  10.3 13.9 %collective-permute-done = f32[2,512,256]{2,1,0:T(8,128)S(1)} collective-permute-done((f32[2,512,256]{2,1,0:T(8,128)S(1)}, f32[2,512,256]{2,1,0:T(8,128)S(1)}, u32[]{:S(2)}, u32[]{:S(2)}) %collective-permute-start) | collective-permute-done | bytes 1048608 | tf_op jit(solution)/shard_map/ppermute | solution.py:19
  25.5 4.9 collective-permute-start.1
  34.2 28.5 %collective-permute-done.1 = f32[2,256,768]{2,1,0:T(8,128)} collective-permute-done((f32[2,256,768]{2,1,0:T(8,128)}, f32[2,256,768]{2,1,0:T(8,128)}, u32[]{:S(2)}, u32[]{:S(2)}) %collective-permute-start.1) | collective-permute-done | bytes 1572896 | tf_op jit(solution)/shard_map/ppermute | solution.py:19
  62.7 3.9 pad_maximum_fusion
  66.7 13.2 %while.51 = (s32[]{:T(128)}, f32[2,768,768]{2,1,0:T(8,128)}, s32[4,3]{1,0:T(4,128)S(1)}, f32[4,2,256,256]{3,2,0,1:T(8,128)S(1)}, s32[]{:T(128)}) while((s32[]{:T(128)}, f32[2,768,768]{2,1,0:T(8,128)}, s32[4,3]{1,0:T(4,128)S(1)}, f32[4,2,256,256]{3,2,0,1:T(8,128)S(1)}, s32[]{:T(128)}) %tuple.177), condition=%wide.while_cond.6, body=%wide.while_body.6.sunk | while | flops 2 | bytes 1048693 | solution.py:50
  121.9 4.3 fusion.51
  131.7 65.1 %while.48 = (s32[]{:T(128)}, f32[3,768,768]{2,1,0:T(8,128)}, s32[4]{0:T(128)S(1)}, s32[4]{0:T(128)S(1)}, f32[4,3,256,256]{3,2,0,1:T(8,128)}, /*index=5*/s32[]{:T(128)}, s32[]{:T(128)}, s32[]{:T(128)}) while((s32[]{:T(128)}, f32[3,768,768]{2,1,0:T(8,128)}, s32[4]{0:T(128)S(1)}, s32[4]{0:T(128)S(1)}, f32[4,3,256,256]{3,2,0,1:T(8,128)}, ...), condition=%wide.region_1.2_spmd, body=%wide.region_0.1_spmd.sunk | while | flops 196616 | bytes 3932353 | solution.py:66
  138.6 9.5 dynamic_update_slice.24
  155.1 9.3 dynamic_update_slice.24
  171.2 9.3 dynamic_update_slice.24
  187.4 9.5 dynamic_update_slice.24
  199.3 25.8 %collective-permute-done.2 = f32[3,768,256]{2,1,0:T(8,128)S(1)} collective-permute-done((f32[3,768,256]{2,1,0:T(8,128)S(1)}, f32[3,768,256]{2,1,0:T(8,128)S(1)}, u32[]{:S(2)}, u32[]{:S(2)}) %collective-permute-start.2) | collective-permute-done | bytes 2359328 | tf_op jit(solution)/shard_map/ppermute | solution.py:19
  232.3 34.5 %collective-permute-done.3 = f32[3,256,512]{2,1,0:T(8,128)S(1)} collective-permute-done((f32[3,256,512]{2,1,0:T(8,128)S(1)}, f32[3,256,512]{2,1,0:T(8,128)S(1)}, u32[]{:S(2)}, u32[]{:S(2)}) %collective-permute-start.3) | collective-permute-done | bytes 1572896 | tf_op jit(solution)/shard_map/ppermute | solution.py:19
  269.5 5.5 collective-permute-start.4
  275.0 13.6 %collective-permute-done.4 = f32[2,512,256]{2,1,0:T(8,128)S(1)} collective-permute-done((f32[2,512,256]{2,1,0:T(8,128)S(1)}, f32[2,512,256]{2,1,0:T(8,128)S(1)}, u32[]{:S(2)}, u32[]{:S(2)}) %collective-permute-start.4) | collective-permute-done | bytes 1048608 | tf_op jit(solution)/shard_map/ppermute | solution.py:19
  291.7 147.1 %all-reduce.11.cloned.1.call-done = (f32[1,256,256]{2,1,0:T(8,128)}, f32[1,256,256]{2,1,0:T(8,128)}, f32[256,256]{1,0:T(8,128)}) async-done(((f32[1,256,256]{2,1,0:T(8,128)}, f32[1,256,256]{2,1,0:T(8,128)}, f32[256,256]{1,0:T(8,128)}), (f32[1,256,256]{2,1,0:T(8,128)}, f32[1,256,256]{2,1,0:T(8,128)}, f32[256,256]{1,0:T(8,128)})) %all-reduce.11.cloned.1.call-update) | async-done | bytes 786448 | tf_op jit(solution)/shard_map/psum | solution.py:115
  441.8 4.0 pad_maximum_fusion.1
  447.3 16.9 %while.52 = (s32[]{:T(128)}, f32[2,768,768]{2,1,0:T(8,128)}, s32[4,3]{1,0:T(4,128)S(1)}, f32[4,2,256,256]{3,2,0,1:T(8,128)}, s32[]{:T(128)}) while((s32[]{:T(128)}, f32[2,768,768]{2,1,0:T(8,128)}, s32[4,3]{1,0:T(4,128)S(1)}, f32[4,2,256,256]{3,2,0,1:T(8,128)}, s32[]{:T(128)}) %tuple.204), condition=%wide.while_cond.7, body=%wide.while_body.7.sunk | while | flops 2 | bytes 1050217 | solution.py:50
  448.0 3.5 bitcast_dynamic-update-slice_fusion.7
  452.1 3.5 bitcast_dynamic-update-slice_fusion.7
  456.2 3.5 bitcast_dynamic-update-slice_fusion.7
  464.2 4.4 fusion.121
  508.0 7.1 fusion.39
  515.2 145.7 %all-reduce.9.cloned.1.call-done = (f32[1,256,256]{2,1,0:T(8,128)}, f32[1,256,256]{2,1,0:T(8,128)}, f32[256,256]{1,0:T(8,128)}) async-done(((f32[1,256,256]{2,1,0:T(8,128)}, f32[1,256,256]{2,1,0:T(8,128)}, f32[256,256]{1,0:T(8,128)}), (f32[1,256,256]{2,1,0:T(8,128)}, f32[1,256,256]{2,1,0:T(8,128)}, f32[256,256]{1,0:T(8,128)})) %all-reduce.9.cloned.1.call-update) | async-done | bytes 786448 | tf_op jit(solution)/shard_map/psum | solution.py:115
  667.4 3.5 broadcast.206.clone.1
  670.9 65.2 %while.49 = (s32[]{:T(128)}, f32[3,768,768]{2,1,0:T(8,128)}, s32[4]{0:T(128)S(1)}, s32[4]{0:T(128)S(1)}, f32[4,3,256,256]{3,2,0,1:T(8,128)}, /*index=5*/s32[]{:T(128)}, s32[]{:T(128)}, s32[]{:T(128)}) while((s32[]{:T(128)}, f32[3,768,768]{2,1,0:T(8,128)}, s32[4]{0:T(128)S(1)}, s32[4]{0:T(128)S(1)}, f32[4,3,256,256]{3,2,0,1:T(8,128)}, ...), condition=%wide.region_9.10_spmd, body=%wide.region_8.9_spmd.sunk | while | flops 196616 | bytes 3932353 | solution.py:66
  677.8 9.6 dynamic_update_slice.25
  694.3 9.2 dynamic_update_slice.25
  710.4 9.2 dynamic_update_slice.25
  726.6 9.5 dynamic_update_slice.25
  738.1 25.8 %collective-permute-done.6 = f32[3,768,256]{2,1,0:T(8,128)S(1)} collective-permute-done((f32[3,768,256]{2,1,0:T(8,128)S(1)}, f32[3,768,256]{2,1,0:T(8,128)S(1)}, u32[]{:S(2)}, u32[]{:S(2)}) %collective-permute-start.6) | collective-permute-done | bytes 2359328 | tf_op jit(solution)/shard_map/ppermute | solution.py:19
  763.8 3.5 add_dynamic-update-slice_fusion.1
  772.3 30.5 %collective-permute-done.7 = f32[3,256,512]{2,1,0:T(8,128)S(1)} collective-permute-done((f32[3,256,512]{2,1,0:T(8,128)S(1)}, f32[3,256,512]{2,1,0:T(8,128)S(1)}, u32[]{:S(2)}, u32[]{:S(2)}) %collective-permute-start.7) | collective-permute-done | bytes 1572896 | tf_op jit(solution)/shard_map/ppermute | solution.py:19
  805.4 6.3 collective-permute-start.8
  811.8 14.9 %collective-permute-done.8 = f32[2,512,256]{2,1,0:T(8,128)S(1)} collective-permute-done((f32[2,512,256]{2,1,0:T(8,128)S(1)}, f32[2,512,256]{2,1,0:T(8,128)S(1)}, u32[]{:S(2)}, u32[]{:S(2)}) %collective-permute-start.8) | collective-permute-done | bytes 1048608 | tf_op jit(solution)/shard_map/ppermute | solution.py:19
  827.9 34.8 %collective-permute-done.9 = f32[2,256,768]{2,1,0:T(8,128)S(1)} collective-permute-done((f32[2,256,768]{2,1,0:T(8,128)}, f32[2,256,768]{2,1,0:T(8,128)S(1)}, u32[]{:S(2)}, u32[]{:S(2)}) %collective-permute-start.9) | collective-permute-done | bytes 1572896 | tf_op jit(solution)/shard_map/ppermute | solution.py:19
  862.7 4.1 pad_maximum_fusion.2
  867.0 13.2 %while.53 = (s32[]{:T(128)}, f32[2,768,768]{2,1,0:T(8,128)}, s32[4,3]{1,0:T(4,128)S(1)}, f32[4,2,256,256]{3,2,0,1:T(8,128)S(1)}, s32[]{:T(128)}) while((s32[]{:T(128)}, f32[2,768,768]{2,1,0:T(8,128)}, s32[4,3]{1,0:T(4,128)S(1)}, f32[4,2,256,256]{3,2,0,1:T(8,128)S(1)}, s32[]{:T(128)}) %tuple.205), condition=%wide.while_cond.8, body=%wide.while_body.8.sunk | while | flops 2 | bytes 1048693 | solution.py:50
  922.2 4.3 fusion.30
  928.5 3.5 broadcast.206
  932.0 66.4 %while.50 = (s32[]{:T(128)}, f32[3,768,768]{2,1,0:T(8,128)}, s32[4]{0:T(128)S(1)}, s32[4]{0:T(128)S(1)}, f32[4,3,256,256]{3,2,0,1:T(8,128)}, /*index=5*/s32[]{:T(128)}, s32[]{:T(128)}, s32[]{:T(128)}) while((s32[]{:T(128)}, f32[3,768,768]{2,1,0:T(8,128)}, s32[4]{0:T(128)S(1)}, s32[4]{0:T(128)S(1)}, f32[4,3,256,256]{3,2,0,1:T(8,128)}, ...), condition=%wide.region_17.18_spmd, body=%wide.region_16.17_spmd.sunk | while | flops 196616 | bytes 3932353 | solution.py:66
  939.2 9.7 dynamic_update_slice.26
  956.0 9.3 dynamic_update_slice.26
  972.4 9.3 dynamic_update_slice.26
  988.8 9.6 dynamic_update_slice.26
  1000.8 25.8 %collective-permute-done.10 = f32[3,768,256]{2,1,0:T(8,128)S(1)} collective-permute-done((f32[3,768,256]{2,1,0:T(8,128)S(1)}, f32[3,768,256]{2,1,0:T(8,128)S(1)}, u32[]{:S(2)}, u32[]{:S(2)}) %collective-permute-start.10) | collective-permute-done | bytes 2359328 | tf_op jit(solution)/shard_map/ppermute | solution.py:19
  1026.6 3.5 add_dynamic-update-slice_fusion
  1032.3 153.2 %all-reduce.7.cloned.1.call-done = (f32[1,256,256]{2,1,0:T(8,128)}, f32[1,256,256]{2,1,0:T(8,128)}, f32[256,256]{1,0:T(8,128)}) async-done(((f32[1,256,256]{2,1,0:T(8,128)}, f32[1,256,256]{2,1,0:T(8,128)}, f32[256,256]{1,0:T(8,128)}), (f32[1,256,256]{2,1,0:T(8,128)}, f32[1,256,256]{2,1,0:T(8,128)}, f32[256,256]{1,0:T(8,128)})) %all-reduce.7.cloned.1.call-update) | async-done | bytes 786448 | tf_op jit(solution)/shard_map/psum | solution.py:115
  (233 shorter events, 258.1 us)
Async XLA Ops:
  7.2 431.6 %all-reduce.11.cloned.1.call-start = ((), (), s32[]{:S(2)}) async-start(), calls=%async_computation.2 | async-start | bytes 1572864 | tf_op jit(solution)/shard_map/psum | solution.py:115
  7.2 2.9 copy-start.3
  8.7 15.5 %collective-permute-start = (f32[2,512,256]{2,1,0:T(8,128)S(1)}, f32[2,512,256]{2,1,0:T(8,128)S(1)}, u32[]{:S(2)}, u32[]{:S(2)}) collective-permute-start(f32[2,512,256]{2,1,0:T(8,128)S(1)} %slice.255), channel_id=1, source_target_pairs={{1,0},{2,1},{3,2},{4,3},{5,4},{6,5},{7,6},{0,7},{9,8},{10,9},{11,1... | collective-permute-start | bytes 3145736 | tf_op jit(solution)/shard_map/ppermute | solution.py:19
  10.3 20.2 %copy-start.22 = (s32[1,1,4,2]{2,3,1,0:T(2,128)S(1)}, s32[1,1,4,2]{2,3,1,0:T(2,128)}, u32[]{:S(2)}) copy-start(s32[1,1,4,2]{2,3,1,0:T(2,128)} %param.26) | copy-start | bytes 100
  25.5 37.1 %collective-permute-start.1 = (f32[2,256,768]{2,1,0:T(8,128)}, f32[2,256,768]{2,1,0:T(8,128)}, u32[]{:S(2)}, u32[]{:S(2)}) collective-permute-start(f32[2,256,768]{2,1,0:T(8,128)} %slice.338), channel_id=1, source_target_pairs={{8,0},{16,8},{24,16},{32,24},{40,32},{48,40},{56,48},{64,56},{72,6... | collective-permute-start | bytes 4718600 | tf_op jit(solution)/shard_map/ppermute | solution.py:19
  66.7 13.2 %copy-start.5 = (f32[256,256]{1,0:T(8,128)S(1)}, f32[256,256]{1,0:T(8,128)}, u32[]{:S(2)}) copy-start(f32[256,256]{1,0:T(8,128)} %get-tuple-element.514) | copy-start | bytes 786436
  96.6 2.7 copy-start.23
  121.9 4.3 copy-start.13
  198.7 26.3 %collective-permute-start.2 = (f32[3,768,256]{2,1,0:T(8,128)S(1)}, f32[3,768,256]{2,1,0:T(8,128)S(1)}, u32[]{:S(2)}, u32[]{:S(2)}) collective-permute-start(f32[3,768,256]{2,1,0:T(8,128)S(1)} %slice.261), channel_id=1, source_target_pairs={{7,0},{0,1},{1,2},{2,3},{3,4},{4,5},{5,6},{6,7},{15,8},{8,9},{9,10... | collective-permute-start | bytes 7077896 | tf_op jit(solution)/shard_map/ppermute | solution.py:19
  230.0 36.9 %collective-permute-start.3 = (f32[3,256,512]{2,1,0:T(8,128)S(1)}, f32[3,256,512]{2,1,0:T(8,128)S(1)}, u32[]{:S(2)}, u32[]{:S(2)}) collective-permute-start(f32[3,256,512]{2,1,0:T(8,128)S(1)} %slice.341), channel_id=1, source_target_pairs={{120,0},{0,8},{8,16},{16,24},{24,32},{32,40},{40,48},{48,56},{56,6... | collective-permute-start | bytes 4718600 | tf_op jit(solution)/shard_map/ppermute | solution.py:19
  232.3 36.4 %copy-start.4 = (f32[2,512,512]{2,1,0:T(8,128)S(1)}, f32[2,512,512]{2,1,0:T(8,128)}, u32[]{:S(2)}) copy-start(f32[2,512,512]{2,1,0:T(8,128)} %param.23) | copy-start | bytes 6291460
  269.5 170.4 %copy-start.6 = (f32[2,256,256]{2,1,0:T(8,128)S(1)}, f32[2,256,256]{2,1,0:T(8,128)}, u32[]{:S(2)}) copy-start(f32[2,256,256]{2,1,0:T(8,128)} %param.24) | copy-start | bytes 1572868
  269.5 19.1 %collective-permute-start.4 = (f32[2,512,256]{2,1,0:T(8,128)S(1)}, f32[2,512,256]{2,1,0:T(8,128)S(1)}, u32[]{:S(2)}, u32[]{:S(2)}) collective-permute-start(f32[2,512,256]{2,1,0:T(8,128)S(1)} %slice.345), channel_id=1, source_target_pairs={{1,0},{2,1},{3,2},{4,3},{5,4},{6,5},{7,6},{0,7},{9,8},{10,9},{11,1... | collective-permute-start | bytes 3145736 | tf_op jit(solution)/shard_map/ppermute | solution.py:19
  288.6 1.5 copy-start.8
  290.1 151.7 %collective-permute-start.5 = (f32[2,256,768]{2,1,0:T(8,128)}, f32[2,256,768]{2,1,0:T(8,128)}, u32[]{:S(2)}, u32[]{:S(2)}) collective-permute-start(f32[2,256,768]{2,1,0:T(8,128)} %pad_maximum_fusion.7), channel_id=1, source_target_pairs={{8,0},{16,8},{24,16},{32,24},{40,32},{48,40},{56,48},{64,56},{72,6... | collective-permute-start | bytes 4718600 | tf_op jit(solution)/shard_map/ppermute | solution.py:19
  291.6 369.3 %all-reduce.9.cloned.1.call-start = ((), (), s32[]{:S(2)}) async-start(), calls=%async_computation.1 | async-start | bytes 1572864 | tf_op jit(solution)/shard_map/psum | solution.py:115
  438.8 3.1 copy-start.9
  439.8 222.1 %copy-start.10 = (f32[256,256]{1,0:T(8,128)}, f32[256,256]{1,0:T(8,128)S(1)}, u32[]{:S(2)}) copy-start(f32[256,256]{1,0:T(8,128)S(1)} %broadcast_add_fusion.2) | copy-start | bytes 786436
  464.2 4.4 copy-start.2
  482.6 2.8 copy-start.24
  515.2 148.3 %copy-start.21 = (f32[256,256]{1,0:T(8,128)S(1)}, f32[256,256]{1,0:T(8,128)}, u32[]{:S(2)}) copy-start(f32[256,256]{1,0:T(8,128)} %get-tuple-element.510) | copy-start | bytes 786436
  515.2 670.3 %all-reduce.7.cloned.1.call-start = ((), (), s32[]{:S(2)}) async-start(), calls=%async_computation | async-start | bytes 1572864 | tf_op jit(solution)/shard_map/psum | solution.py:115
  661.9 2.8 copy-start.18
  663.4 1.3 copy-start.14
  663.4 1.9 copy-start.15
  737.9 25.9 %collective-permute-start.6 = (f32[3,768,256]{2,1,0:T(8,128)S(1)}, f32[3,768,256]{2,1,0:T(8,128)S(1)}, u32[]{:S(2)}, u32[]{:S(2)}) collective-permute-start(f32[3,768,256]{2,1,0:T(8,128)S(1)} %slice.274), channel_id=1, source_target_pairs={{7,0},{0,1},{1,2},{2,3},{3,4},{4,5},{5,6},{6,7},{15,8},{8,9},{9,10... | collective-permute-start | bytes 7077896 | tf_op jit(solution)/shard_map/ppermute | solution.py:19
  768.9 33.9 %collective-permute-start.7 = (f32[3,256,512]{2,1,0:T(8,128)S(1)}, f32[3,256,512]{2,1,0:T(8,128)S(1)}, u32[]{:S(2)}, u32[]{:S(2)}) collective-permute-start(f32[3,256,512]{2,1,0:T(8,128)S(1)} %slice.349), channel_id=1, source_target_pairs={{120,0},{0,8},{8,16},{16,24},{24,32},{32,40},{40,48},{48,56},{56,6... | collective-permute-start | bytes 4718600 | tf_op jit(solution)/shard_map/ppermute | solution.py:19
  805.3 22.6 %copy-start = (f32[2,512,512]{2,1,0:T(8,128)}, f32[2,512,512]{2,1,0:T(8,128)S(1)}, u32[]{:S(2)}) copy-start(f32[2,512,512]{2,1,0:T(8,128)S(1)} %fusion.1) | copy-start | bytes 6291460
  805.4 21.2 %collective-permute-start.8 = (f32[2,512,256]{2,1,0:T(8,128)S(1)}, f32[2,512,256]{2,1,0:T(8,128)S(1)}, u32[]{:S(2)}, u32[]{:S(2)}) collective-permute-start(f32[2,512,256]{2,1,0:T(8,128)S(1)} %slice.353), channel_id=1, source_target_pairs={{1,0},{2,1},{3,2},{4,3},{5,4},{6,5},{7,6},{0,7},{9,8},{10,9},{11,1... | collective-permute-start | bytes 3145736 | tf_op jit(solution)/shard_map/ppermute | solution.py:19
  827.9 34.8 %collective-permute-start.9 = (f32[2,256,768]{2,1,0:T(8,128)}, f32[2,256,768]{2,1,0:T(8,128)S(1)}, u32[]{:S(2)}, u32[]{:S(2)}) collective-permute-start(f32[2,256,768]{2,1,0:T(8,128)} %pad_maximum_fusion.6), channel_id=1, source_target_pairs={{8,0},{16,8},{24,16},{32,24},{40,32},{48,40},{56,48},{64,56},{72,6... | collective-permute-start | bytes 4718600 | tf_op jit(solution)/shard_map/ppermute | solution.py:19
  896.8 2.7 copy-start.25
  922.2 4.3 copy-start.12
  1000.3 26.3 %collective-permute-start.10 = (f32[3,768,256]{2,1,0:T(8,128)S(1)}, f32[3,768,256]{2,1,0:T(8,128)S(1)}, u32[]{:S(2)}, u32[]{:S(2)}) collective-permute-start(f32[3,768,256]{2,1,0:T(8,128)S(1)} %slice.287), channel_id=1, source_target_pairs={{7,0},{0,1},{1,2},{2,3},{3,4},{4,5},{5,6},{6,7},{15,8},{8,9},{9,10... | collective-permute-start | bytes 7077896 | tf_op jit(solution)/shard_map/ppermute | solution.py:19
  1030.1 156.4 %copy-start.7 = (f32[2,256,256]{2,1,0:T(8,128)S(1)}, f32[2,256,256]{2,1,0:T(8,128)}, u32[]{:S(2)}) copy-start(f32[2,256,256]{2,1,0:T(8,128)} %param.24) | copy-start | bytes 1572868
  1030.1 156.4 %copy-start.11 = (f32[256,256]{1,0:T(8,128)S(1)}, f32[256,256]{1,0:T(8,128)}, u32[]{:S(2)}) copy-start(f32[256,256]{1,0:T(8,128)} %copy-done.10) | copy-start | bytes 786436
  1030.1 156.4 %copy-start.16 = (f32[1,256,256]{2,1,0:T(8,128)S(1)}, f32[1,256,256]{2,1,0:T(8,128)}, u32[]{:S(2)}) copy-start(f32[1,256,256]{2,1,0:T(8,128)} %get-tuple-element.479) | copy-start | bytes 786436
  1030.1 156.4 %copy-start.17 = (f32[1,256,256]{2,1,0:T(8,128)S(1)}, f32[1,256,256]{2,1,0:T(8,128)}, u32[]{:S(2)}) copy-start(f32[1,256,256]{2,1,0:T(8,128)} %get-tuple-element.480) | copy-start | bytes 786436
  1030.1 156.4 %copy-start.19 = (f32[256,256]{1,0:T(8,128)S(1)}, f32[256,256]{1,0:T(8,128)}, u32[]{:S(2)}) copy-start(f32[256,256]{1,0:T(8,128)} %copy-done.18) | copy-start | bytes 786436
  1030.1 156.4 %copy-start.20 = (f32[1,256,256]{2,1,0:T(8,128)S(1)}, f32[1,256,256]{2,1,0:T(8,128)}, u32[]{:S(2)}) copy-start(f32[1,256,256]{2,1,0:T(8,128)} %get-tuple-element.476) | copy-start | bytes 786436
  1031.8 159.1 %collective-permute-start.11 = (f32[3,256,512]{2,1,0:T(8,128)S(1)}, f32[3,256,512]{2,1,0:T(8,128)}, u32[]{:S(2)}, u32[]{:S(2)}) collective-permute-start(f32[3,256,512]{2,1,0:T(8,128)S(1)} %slice.357), channel_id=1, source_target_pairs={{120,0},{0,8},{8,16},{16,24},{24,32},{32,40},{40,48},{48,56},{56,6... | collective-permute-start | bytes 4718600 | tf_op jit(solution)/shard_map/ppermute | solution.py:19
  1190.9 2.5 copy-start.1
Sparse Core Ops, SparseCore 0:
  291.7 146.9 all-reduce.10
  515.3 145.5 all-reduce.8
  1032.5 153.0 all-reduce.6
where the time goes:
time: 1220 us; the launch traced here: 1200 us
  waiting for transfers between devices  694 us (57%)
  local copies, waits for them, and re-layouts  203 us (17%)
  matrix products  143 us (12%)
  other arithmetic  75.3 us (6%)
  loops' own time  48.2 us (4%)
  starting transfers between devices  22.7 us (2%)
  between operations  15.4 us (1%)
    psum x3, waiting for transfers between devices, shards(): lax.psum((grad_re, grad_im, power_sum), ('row', 'col'))  446 us
    ppermute x12, waiting for transfers between devices, passed_along(): return lax.ppermute(block, axis, route)  248 us
    dynamic_update_slice x12, local copies, waits for them, and re-layouts, add_one(): lax.dynamic_update_slice(running, current + pieces[slot_index], corner_at)  113 us
    dot_general x24, matrix products, on_right(): return jnp.einsum('pjk,kl->pjl', operand, matrix, precision=highest)  74.5 us
    dot_general x24, matrix products, on_left(): return jnp.einsum('jk,pkl->pjl', matrix, operand, precision=highest)  68.6 us
    another operation x3, loops' own time, deposit(): return lax.fori_loop(0, pieces.shape[0], add_one, canvas)  47.3 us
    gather x36, local copies, waits for them, and re-layouts  42.3 us
  transfers between devices with their start and end apart: 15, of which 13 were waited for; matrix products, arithmetic and copies ran while one was open for 1% of the time, Pallas kernels for 0%

commit v1 on v0

v1 whole, which is shorter than its diff:
```python
import math

import jax
import jax.numpy as jnp
import numpy as np
from jax import lax
from jax.experimental import pallas as pl
from jax.experimental.pallas import tpu as pltpu
from jax.sharding import PartitionSpec as P

PASSES = 3
F = 256
TILE = 512
WIDE = TILE + F
HALF = F // 2
LANES = 128

amp_floor = 0.1
object_damping = 0.5
probe_damping = 1.0

VMEM = pl.BlockSpec(memory_space=pltpu.VMEM)
SMEM = pl.BlockSpec(memory_space=pltpu.SMEM)


def passed_along(block, axis, distance):
    size = lax.axis_size(axis)
    route = [((i - distance) % size, i) for i in range(size)]
    return lax.ppermute(block, axis, route)


def split(x):
    high = x.astype(jnp.bfloat16)
    low = (x - high.astype(jnp.float32)).astype(jnp.bfloat16)
    return high, low


def tables():
    k = np.arange(F)
    angles = (k[:, None] * k[None, :] % F) * (-2.0 * math.pi / F)
    re = np.cos(angles) / math.sqrt(F)
    im = np.sin(angles) / math.sqrt(F)
    left = np.block([[re, -im], [im, re]]).astype(np.float32)
    right = np.block([[re, im], [-im, re]]).astype(np.float32)

    def terms(m):
        high = m.astype(jnp.bfloat16)
        low = (m - high.astype(np.float32)).astype(jnp.bfloat16)
        return high, low

    lh, ll = terms(left)
    rh, rl = terms(right)
    return np.concatenate([lh, lh, ll], 1), np.concatenate([rh, rh, rl], 0)


def transform(re, im, left, right):
    h, l = split(jnp.concatenate([re, im], 0))
    y = jnp.dot(left[...], jnp.concatenate([h, l, h], 0), preferred_element_type=jnp.float32)
    h, l = split(jnp.concatenate([y[:F], y[F:]], 1))
    z = jnp.dot(jnp.concatenate([h, l, h], 1), right[...], preferred_element_type=jnp.float32)
    return z[:, :F], z[:, F:]


def window(ref, lead, r, c):
    r0 = pl.multiple_of((r // 8) * 8, 8)
    c0 = pl.multiple_of((c // LANES) * LANES, LANES)
    rs, cs = r - r0, c - c0
    w = ref[lead + (pl.ds(r0, F + 8), pl.ds(c0, F + LANES))]
    lane = lax.broadcasted_iota(jnp.int32, (F + 8, LANES), 1)
    back = lax.rem(LANES - cs, LANES)
    t = [pltpu.roll(w[:, i * LANES : (i + 1) * LANES], back, 1) for i in range(3)]
    w = jnp.concatenate([jnp.where(lane < LANES - cs, t[i], t[i + 1]) for i in range(2)], 1)
    w = pltpu.roll(w.reshape(F // 8 + 1, 8, F), lax.rem(8 - rs, 8), 1)
    sub = lax.broadcasted_iota(jnp.int32, (F // 8, 8, F), 1)
    return jnp.where(sub < 8 - rs, w[:-1], w[1:]).reshape(F, F)


def deposit(ref, lead, r, c, x):
    r0 = pl.multiple_of((r // 8) * 8, 8)
    c0 = pl.multiple_of((c // LANES) * LANES, LANES)
    rs, cs = r - r0, c - c0
    w = pltpu.roll(x.reshape(F // 8, 8, F), rs, 1)
    zero = jnp.zeros((1, 8, F), jnp.float32)
    sub = lax.broadcasted_iota(jnp.int32, (F // 8 + 1, 8, F), 1)
    w = jnp.where(sub >= rs, jnp.concatenate([w, zero], 0), jnp.concatenate([zero, w], 0))
    w = w.reshape(F + 8, F)
    lane = lax.broadcasted_iota(jnp.int32, (F + 8, LANES), 1)
    a = pltpu.roll(w[:, :LANES], cs, 1)
    b = pltpu.roll(w[:, LANES:], cs, 1)
    t = [jnp.where(lane >= cs, a, 0.0), jnp.where(lane >= cs, b, a), jnp.where(lane >= cs, 0.0, b)]
    at = lead + (pl.ds(r0, F + 8), pl.ds(c0, F + LANES))
    ref[at] = ref[at] + jnp.concatenate(t, 1)


def visit_frames(info, amplitude, left, right, ob, pr, canvas, glow, grads):
    canvas[...] = jnp.zeros_like(canvas)
    glow[F : F + WIDE, F : F + WIDE] = jnp.zeros((WIDE, WIDE), jnp.float32)
    grads[...] = jnp.zeros_like(grads)

    def own(k, carry):
        r, c = info[4, k], info[4, 4 + k]
        fr = window(ob, (0,), r, c)
        fi = window(ob, (1,), r, c)
        qr, qi = pr[0], pr[1]
        zr, zi = transform(qr * fr - qi * fi, qr * fi + qi * fr, left, right)
        power = zr * zr + zi * zi
        ratio = amplitude[k] * lax.rsqrt(jnp.maximum(power, amp_floor * amp_floor)) - 1.0
        br, bi = transform(zr * ratio, -(zi * ratio), left, right)
        grads[0] += fr * br - fi * bi
        grads[1] += -(fr * bi) - fi * br
        grads[2] += fr * fr + fi * fi
        deposit(canvas, (0,), r, c, qr * br - qi * bi)
        deposit(canvas, (1,), r, c, -(qr * bi) - qi * br)
        return carry

    lax.fori_loop(0, info[4, 8], own, 0)

    def near(i, carry):
        n, k = i // 4, lax.rem(i, 4)
        r = info[n, k] + TILE * (n // 3) - (TILE - F)
        c = info[n, 4 + k] + TILE * lax.rem(n, 3) - (TILE - F)
        live = k < info[n, 8]
        meets = (r > 0) & (r < F + WIDE) & (c > 0) & (c < F + WIDE)

        @pl.when(live & meets)
        def _():
            deposit(glow, (), r, c, pr[0] * pr[0] + pr[1] * pr[1])

        return carry

    lax.fori_loop(0, 36, near, 0)


def hand_out(canvas, glow, grads, l_out, zl_out, zr_out, up_out, dn_out, g_out):
    l_out[...] = glow[F : F + WIDE, F : F + WIDE]
    zl_out[...] = canvas[:, :, :F]
    zr_out[...] = canvas[:, :, TILE:]
    up_out[...] = canvas[:, :F, F:TILE]
    dn_out[...] = canvas[:, TILE:, F:TILE]
    for p in range(3):
        for h in range(2):
            for t in range(2):
                g_out[pl.ds(4 * p + 2 * t + h, HALF, stride=16), :] = grads[p, h * HALF : (h + 1) * HALF, t * LANES : (t + 1) * LANES]
    for j in range(12, 16):
        g_out[pl.ds(j, HALF, stride=16), :] = jnp.zeros((HALF, LANES), jnp.float32)


def first_kernel(info, amp, left, right, probe, tile, below, beside, corner, *rest):
    (ob, canvas), outs, (pr, glow, grads) = rest[:2], rest[2:8], rest[8:]
    ob[:, :TILE, :TILE] = tile[...]
    ob[:, TILE:, :TILE] = below[...]
    ob[:, :TILE, TILE:] = beside[...]
    ob[:, TILE:, TILE:] = corner[...]
    pr[...] = probe[...]
    visit_frames(info, amp, left, right, ob, pr, canvas, glow, grads)
    hand_out(canvas, glow, grads, *outs)


def gathered_probe(pg, pr):
    for p in range(2):
        for h in range(2):
            for t in range(2):
                pr[p, h * HALF : (h + 1) * HALF, t * LANES : (t + 1) * LANES] = pg[pl.ds(4 * p + 2 * t + h, HALF, stride=8), :]


def refreshed(put, size, o, n, l, zl, zr, cup, cdn, sup, sdn):
    for i in range(size // F):
        for j in range(size // F):
            rows, cols = slice(i * F, (i + 1) * F), slice(j * F, (j + 1) * F)
            scale = 1.0 / (l[rows, cols] + object_damping)
            for p in range(2):
                s = n[p, rows, cols]
                if j == 0:
                    s = s + zl[p, rows, :]
                if j == 2:
                    s = s + zr[p, rows, :]
                if i == 0:
                    s = s + (cdn[p] if j == 1 else sdn[j // 2, p])
                if i == 2:
                    s = s + (cup[p] if j == 1 else sup[j // 2, p])
                put(p, rows, cols, o[p, rows, cols] + s * scale)


def next_kernel(info, amp, left, right, pg, o, n, l, zl, zr, cup, cdn, sup, sdn, *rest):
    (ob, canvas), outs, (pr, glow, grads) = rest[:2], rest[2:8], rest[8:]

    def put(p, rows, cols, value):
        ob[p, rows, cols] = value

    refreshed(put, WIDE, o, n, l, zl, zr, cup, cdn, sup, sdn)
    gathered_probe(pg, pr)
    visit_frames(info, amp, left, right, ob, pr, canvas, glow, grads)
    hand_out(canvas, glow, grads, *outs)


def last_kernel(pg, o, n, l, zl, cdn, sdn, o_out, p_out):
    def put(p, rows, cols, value):
        o_out[p, rows, cols] = value

    refreshed(put, TILE, o, n, l, zl, None, None, cdn, None, sdn)
    gathered_probe(pg, p_out)


def probe_kernel(g, old, new, spread):
    s = jnp.sum(g[...].reshape(HALF, 16, LANES), axis=0)
    value = old[...] + s[:8] / (jnp.concatenate([s[8:12], s[8:12]], 0) + probe_damping)
    new[...] = value
    spread[...] = jnp.broadcast_to(value[None], (HALF, 8, LANES)).reshape(HALF * 8, LANES)


def f32(*shape):
    return jax.ShapeDtypeStruct(shape, jnp.float32)


PARAMS = pltpu.CompilerParams(vmem_limit_bytes=48 << 20)


def call_frames(kernel, *args):
    scratch = [
        pltpu.VMEM((2, F, F), jnp.float32),
        pltpu.VMEM((WIDE + 2 * F, WIDE + 2 * F), jnp.float32),
        pltpu.VMEM((3, F, F), jnp.float32),
    ]
    outs = (
        f32(2, WIDE, WIDE), f32(2, WIDE, WIDE), f32(WIDE, WIDE),
        f32(2, WIDE, F), f32(2, WIDE, F), f32(2, F, F), f32(2, F, F), f32(HALF * 16, LANES),
    )
    return pl.pallas_call(
        kernel,
        out_shape=outs,
        in_specs=[SMEM] + [VMEM] * (len(args) - 1),
        out_specs=[VMEM] * len(outs),
        scratch_shapes=scratch,
        compiler_params=PARAMS,
    )(*args)


def everyone(x):
    return lax.all_to_all(x, ("row", "col"), 0, 0)


def shards(object_field, probe, amplitude, positions, counts):
    me = lax.axis_index(("row", "col"))
    left, right = (jnp.asarray(t) for t in tables())
    amp = amplitude[0, 0]
    mine = jnp.concatenate([positions[0, 0, :, 0], positions[0, 0, :, 1], counts[0], jnp.zeros((7,), jnp.int32)])[None]

    below = passed_along(object_field[:, :F, :], "row", -1)
    beside = passed_along(object_field[:, :, :F], "col", -1)
    info = jnp.concatenate([passed_along(mine, "col", 1), mine, passed_along(mine, "col", -1)], 0)
    info = jnp.concatenate([passed_along(info, "row", 1), info, passed_along(info, "row", -1)], 0)
    corner = passed_along(below[:, :, :F], "col", -1)

    own = lax.dynamic_slice(probe.reshape(2, 2, HALF, 2, LANES), (0, 0, me, 0, 0), (2, 2, 1, 2, LANES))
    own = own[:, :, 0].transpose(0, 2, 1, 3).reshape(8, LANES)

    state = call_frames(first_kernel, info, amp, left, right, probe, object_field, below, beside, corner)
    for sweep in range(PASSES):
        last = sweep == PASSES - 1
        ob, numer, light, to_left, to_right, up, down, grad = state
        grad = grad.reshape(HALF, 16, LANES)
        from_left = passed_along(to_right, "col", 1)
        centre_down = passed_along(down, "row", 1)
        if not last:
            from_right = passed_along(to_left, "col", -1)
            centre_up = passed_along(up, "row", -1)
        to_left, to_right, up, down, grad = lax.optimization_barrier((to_left, to_right, up, down, grad))
        grad = everyone(grad)
        grad, from_left = lax.optimization_barrier((grad, from_left))
        own, spread = pl.pallas_call(
            probe_kernel, out_shape=(f32(8, LANES), f32(HALF * 8, LANES)),
            in_specs=[VMEM] * 2, out_specs=[VMEM] * 2, compiler_params=PARAMS,
        )(grad.reshape(HALF * 16, LANES), own)
        spread = spread.reshape(HALF, 8, LANES)
        if last:
            side_down = (numer[:, TILE:, :F] + from_left[:, TILE:])[None]
            sides = (side_down,)
            got = (passed_along(side_down, "row", 1),)
        else:
            side_up = jnp.stack([numer[:, :F, :F] + from_left[:, :F], numer[:, :F, TILE:] + from_right[:, :F]])
            side_down = jnp.stack([numer[:, TILE:, :F] + from_left[:, TILE:], numer[:, TILE:, TILE:] + from_right[:, TILE:]])
            sides = (side_up, side_down)
            got = (passed_along(side_up, "row", -1), passed_along(side_down, "row", 1))
        sides, spread = lax.optimization_barrier((sides, spread))
        pg = everyone(spread).reshape(HALF * 8, LANES)
        if last:
            return pl.pallas_call(
                last_kernel, out_shape=(f32(2, TILE, TILE), f32(2, F, F)),
                in_specs=[VMEM] * 7, out_specs=[VMEM] * 2, compiler_params=PARAMS,
            )(pg, ob, numer, light, from_left, centre_down, got[0])
        state = call_frames(
            next_kernel, info, amp, left, right, pg, ob, numer, light,
            from_left, from_right, centre_up, centre_down, got[0], got[1],
        )


def solution(mesh):
    return jax.shard_map(
        shards,
        mesh=mesh,
        in_specs=(
            P(None, "row", "col"),
            P(),
            P("row", "col", None, None, None),
            P("row", "col", None, None),
            P("row", "col"),
        ),
        out_specs=(P(None, "row", "col"), P()),
        check_vma=False,
    )
```

time: 1220 us -> 387 us (0.32); the launches traced: 1200 us -> 388 us
  waiting for transfers between devices: 694 us -> 137 us
  local copies, waits for them, and re-layouts: 203 us -> 9.48 us
  matrix products: 143 us -> 0 us
  Pallas kernels: 0 us -> 76.9 us
  blocking collectives: 0 us -> 64 us
  starting transfers between devices: 22.7 us -> 86.4 us
  other arithmetic: 75.3 us -> 12.2 us
  loops' own time: 48.2 us -> 0 us
  between operations: 15.4 us -> 1.54 us
    psum x3 -> x0, waiting for transfers between devices: 446 us -> none  [shards(): lax.psum((grad_re, grad_im, power_sum), ('row', 'col'))]
    ppermute x12 -> x22, waiting for transfers between devices: 248 us -> 84 us  [passed_along(): return lax.ppermute(block, axis, route)]
    dot_general x48 -> x0, matrix products: 143 us -> none  [the longest x24 74.5 us: on_right(): return jnp.einsum('pjk,kl->pjl', operand, matrix, precision=highest)]
    dynamic_update_slice x12 -> x0, local copies, waits for them, and re-layouts: 113 us -> none  [add_one(): lax.dynamic_update_slice(running, current + pieces[slot_index], corner_at)]
    pallas_call x0 -> x7, Pallas kernels: none -> 76.9 us  [the longest x3 68.5 us: call_frames(): pl.pallas_call(kernel, out_shape=outs, in_specs=[SMEM] + [VMEM] * (len(ar...]
    all_to_all x0 -> x2, blocking collectives: none -> 64 us  [everyone(): return lax.all_to_all(x, ('row', 'col'), 0, 0)]
    all_to_all x0 -> x4, waiting for transfers between devices: none -> 53.1 us  [everyone(): return lax.all_to_all(x, ('row', 'col'), 0, 0)]
    another operation x6 -> x0, loops' own time: 48.2 us -> none  [the longest x3 47.3 us: deposit(): return lax.fori_loop(0, pieces.shape[0], add_one, canvas)]
  transfers between devices with their start and end apart: 15 -> 26, of which waited for: 13 -> 12; matrix products, arithmetic and copies ran while one was open for 1% -> 2% of each run, Pallas kernels for 0% -> 1%
where the time goes in v1:
time: 387 us; the launch traced here: 388 us
  waiting for transfers between devices  137 us (35%)
  starting transfers between devices  86.4 us (22%)
  Pallas kernels  76.9 us (20%)
  blocking collectives  64 us (17%)
  other arithmetic  12.2 us (3%)
  local copies, waits for them, and re-layouts  9.48 us (2%)
    ppermute x22, waiting for transfers between devices, passed_along(): return lax.ppermute(block, axis, route)  84 us
    pallas_call x3, Pallas kernels, call_frames(): pl.pallas_call(kernel, out_shape=outs, in_specs=[SMEM] + [VMEM] * (len(ar...  68.5 us
    all_to_all x2, blocking collectives, everyone(): return lax.all_to_all(x, ('row', 'col'), 0, 0)  64 us
    all_to_all x4, waiting for transfers between devices, everyone(): return lax.all_to_all(x, ('row', 'col'), 0, 0)  53.1 us
    ppermute x22, starting transfers between devices, passed_along(): return lax.ppermute(block, axis, route)  47 us
    all_to_all x4, starting transfers between devices, everyone(): return lax.all_to_all(x, ('row', 'col'), 0, 0)  39.4 us
    another operation x4, other arithmetic, shards(): jnp.stack([numer[:, TILE:, :F] + from_left[:, TILE:], numer[:, TILE:, TIL...  8.11 us
  transfers between devices with their start and end apart: 26, of which 12 were waited for; matrix products, arithmetic and copies ran while one was open for 2% of the time, Pallas kernels for 1%

profile of v1, /device:TPU:1, one launch (start us, length us, event | category | flops | bytes accessed | tf_op | source)
XLA Modules:
  0.0 387.6 jit_solution(11622207524808555143)
XLA Ops:
  0.6 1.4 slice.71
  2.1 5.8 %collective-permute-start.4 = (f32[2,256,512]{2,1,0:T(8,128)S(1)}, f32[2,256,512]{2,1,0:T(8,128)S(1)}, u32[]{:S(2)}, u32[]{:S(2)}) collective-permute-start(f32[2,256,512]{2,1,0:T(8,128)S(1)} %slice.71), channel_id=1, source_target_pairs={{8,0},{16,8},{24,16},{32,24},{40,32},{48,40},{56,48},{64,56},{72,6... | collective-permute-start | bytes 3145736 | tf_op jit(solution)/shard_map/ppermute | solution.py:29
  8.0 1.1 slice.72
  9.0 1.0 collective-permute-start.5
  10.0 19.8 %collective-permute-done.4.below = f32[2,256,512]{2,1,0:T(8,128)S(1)} collective-permute-done((f32[2,256,512]{2,1,0:T(8,128)S(1)}, f32[2,256,512]{2,1,0:T(8,128)S(1)}, u32[]{:S(2)}, u32[]{:S(2)}) %collective-permute-start.4) | collective-permute-done | bytes 1048608 | tf_op jit(solution)/shard_map/ppermute | solution.py:29
  29.8 0.8 slice.92
  30.6 1.5 collective-permute-start.6
  32.9 2.6 collective-permute-start.1
  35.5 5.3 %collective-permute-done.1 = s32[1,16]{1,0:T(1,128)S(1)} collective-permute-done((s32[1,16]{1,0:T(1,128)S(1)}, s32[1,16]{1,0:T(1,128)S(1)}, u32[]{:S(2)}, u32[]{:S(2)}) %collective-permute-start.1) | collective-permute-done | bytes 96 | tf_op jit(solution)/shard_map/ppermute | solution.py:29
  40.9 5.6 %collective-permute-start.3 = (s32[3,16]{1,0:T(4,128)S(1)}, s32[3,16]{1,0:T(4,128)S(1)}, u32[]{:S(2)}, u32[]{:S(2)}) collective-permute-start(s32[3,16]{1,0:T(4,128)S(1)} %pad_add_fusion), channel_id=1, source_target_pairs={{8,0},{16,8},{24,16},{32,24},{40,32},{48,40},{56,48},{64,56},{72,6... | collective-permute-start | bytes 584 | tf_op jit(solution)/shard_map/ppermute | solution.py:29
  47.2 5.0 %collective-permute-done.2 = s32[3,16]{1,0:T(4,128)S(1)} collective-permute-done((s32[3,16]{1,0:T(4,128)S(1)}, s32[3,16]{1,0:T(4,128)S(1)}, u32[]{:S(2)}, u32[]{:S(2)}) %collective-permute-start.2) | collective-permute-done | bytes 224 | tf_op jit(solution)/shard_map/ppermute | solution.py:29
  52.4 19.6 %shard_map.86 = (f32[2,768,768]{2,1,0:T(8,128)}, f32[2,768,768]{2,1,0:T(8,128)}, f32[768,768]{1,0:T(8,128)}, f32[2,768,256]{2,1,0:T(8,128)}, f32[2,768,256]{2,1,...) custom-call(s32[9,16]{1,0:T(8,128)S(1)} %concatenate.12.info, ...), custom_call_target="tpu_custom_call" | custom-call | tf_op jit(solution)/shard_map/pallas_call | solution.py:228
  72.0 10.7 %collective-permute-start.8 = (f32[2,768,256]{2,1,0:T(8,128)}, f32[2,768,256]{2,1,0:T(8,128)S(1)}, u32[]{:S(2)}, u32[]{:S(2)}) collective-permute-start(f32[2,768,256]{2,1,0:T(8,128)} %get-tuple-element.42), channel_id=1, source_target_pairs={{1,0},{2,1},{3,2},{4,3},{5,4},{6,5},{7,6},{0,7},{9,8},{10,9},{11,1... | collective-permute-start | bytes 4718600 | tf_op jit(solution)/shard_map/ppermute | solution.py:29
  82.7 32.0 %all_to_all.30 = f32[128,16,128]{2,1,0:T(8,128)S(1)} all-to-all(f32[128,16,128]{2,1,0:T(8,128)S(1)} %bitcast.55), channel_id=1, replica_groups=mesh['row'=16,'col'=8] {'row','col'}, dimensions={0} | all-to-all | bytes 2097152 | tf_op jit(solution)/shard_map/all_to_all | solution.py:239
  114.7 3.0 add_bitcast_fusion.3
  117.7 1.0 pad_maximum_fusion
  118.8 1.1 pad_maximum_fusion.1
  119.8 1.5 collective-permute-start.12
  121.3 1.1 reshape.48
  122.3 3.3 collective-permute-start.9
  126.4 1.0 shard_map.87
  127.3 10.1 %all-to-all-start.1 = ((f32[128,8,128]{2,1,0:T(8,128)}), f32[128,8,128]{2,1,0:T(8,128)S(1)}, u32[]{:S(2)}, u32[]{:S(2)}) async-start(f32[128,8,128]{2,1,0:T(8,128)} %bitcast.14), calls=%async_computation.1 | async-start | bytes 1048576 | tf_op jit(solution)/shard_map/all_to_all | solution.py:239
  137.5 17.2 %collective-permute-done.9.cup = f32[2,256,256]{2,1,0:T(8,128)S(1)} collective-permute-done((f32[2,256,256]{2,1,0:T(8,128)}, f32[2,256,256]{2,1,0:T(8,128)S(1)}, u32[]{:S(2)}, u32[]{:S(2)}) %collective-permute-start.9) | collective-permute-done | bytes 524320 | tf_op jit(solution)/shard_map/ppermute | solution.py:29
  154.7 8.6 %collective-permute-done.10.cdn = f32[2,256,256]{2,1,0:T(8,128)} collective-permute-done((f32[2,256,256]{2,1,0:T(8,128)}, f32[2,256,256]{2,1,0:T(8,128)}, u32[]{:S(2)}, u32[]{:S(2)}) %collective-permute-start.10) | collective-permute-done | bytes 524320 | tf_op jit(solution)/shard_map/ppermute | solution.py:29
  163.2 6.2 %all-to-all-done.1 = f32[128,8,128]{2,1,0:T(8,128)S(1)} async-done(((f32[128,8,128]{2,1,0:T(8,128)}), f32[128,8,128]{2,1,0:T(8,128)S(1)}, u32[]{:S(2)}, u32[]{:S(2)}) %all-to-all-start.1) | async-done | bytes 524320 | tf_op jit(solution)/shard_map/all_to_all | solution.py:239
  169.4 24.8 %shard_map.88 = (f32[2,768,768]{2,1,0:T(8,128)}, f32[2,768,768]{2,1,0:T(8,128)}, f32[768,768]{1,0:T(8,128)}, f32[2,768,256]{2,1,0:T(8,128)}, f32[2,768,256]{2,1,...) custom-call(s32[9,16]{1,0:T(8,128)S(1)} %concatenate.12.info, ...), custom_call_target="tpu_custom_call" | custom-call | tf_op jit(solution)/shard_map/pallas_call | solution.py:228
  194.2 8.7 %collective-permute-start.14 = (f32[2,768,256]{2,1,0:T(8,128)}, f32[2,768,256]{2,1,0:T(8,128)S(1)}, u32[]{:S(2)}, u32[]{:S(2)}) collective-permute-start(f32[2,768,256]{2,1,0:T(8,128)} %get-tuple-element.55), channel_id=1, source_target_pairs={{1,0},{2,1},{3,2},{4,3},{5,4},{6,5},{7,6},{0,7},{9,8},{10,9},{11,1... | collective-permute-start | bytes 4718600 | tf_op jit(solution)/shard_map/ppermute | solution.py:29
  202.9 32.0 %all_to_all.31 = f32[128,16,128]{2,1,0:T(8,128)S(1)} all-to-all(f32[128,16,128]{2,1,0:T(8,128)S(1)} %bitcast.54), channel_id=1, replica_groups=mesh['row'=16,'col'=8] {'row','col'}, dimensions={0} | all-to-all | bytes 2097152 | tf_op jit(solution)/shard_map/all_to_all | solution.py:239
  235.0 3.0 add_bitcast_fusion.1
  238.0 1.1 pad_maximum_fusion.2
  239.0 1.1 pad_maximum_fusion.3
  240.1 1.5 collective-permute-start.18
  241.6 3.3 collective-permute-start.15
  244.9 1.0 shard_map.89
  245.9 10.1 %all-to-all-start.3 = ((f32[128,8,128]{2,1,0:T(8,128)}), f32[128,8,128]{2,1,0:T(8,128)S(1)}, u32[]{:S(2)}, u32[]{:S(2)}) async-start(f32[128,8,128]{2,1,0:T(8,128)} %bitcast.22), calls=%async_computation.3 | async-start | bytes 1048576 | tf_op jit(solution)/shard_map/all_to_all | solution.py:239
  256.0 18.9 %collective-permute-done.15.cup = f32[2,256,256]{2,1,0:T(8,128)S(1)} collective-permute-done((f32[2,256,256]{2,1,0:T(8,128)}, f32[2,256,256]{2,1,0:T(8,128)S(1)}, u32[]{:S(2)}, u32[]{:S(2)}) %collective-permute-start.15) | collective-permute-done | bytes 524320 | tf_op jit(solution)/shard_map/ppermute | solution.py:29
  274.9 8.4 %collective-permute-done.16.cdn = f32[2,256,256]{2,1,0:T(8,128)} collective-permute-done((f32[2,256,256]{2,1,0:T(8,128)}, f32[2,256,256]{2,1,0:T(8,128)}, u32[]{:S(2)}, u32[]{:S(2)}) %collective-permute-start.16) | collective-permute-done | bytes 524320 | tf_op jit(solution)/shard_map/ppermute | solution.py:29
  283.4 5.9 %all-to-all-done.3 = f32[128,8,128]{2,1,0:T(8,128)S(1)} async-done(((f32[128,8,128]{2,1,0:T(8,128)}), f32[128,8,128]{2,1,0:T(8,128)S(1)}, u32[]{:S(2)}, u32[]{:S(2)}) %all-to-all-start.3) | async-done | bytes 524320 | tf_op jit(solution)/shard_map/all_to_all | solution.py:239
  289.2 24.1 %shard_map.90 = (f32[2,768,768]{2,1,0:T(8,128)}, f32[2,768,768]{2,1,0:T(8,128)}, f32[768,768]{1,0:T(8,128)}, f32[2,768,256]{2,1,0:T(8,128)}, f32[2,768,256]{2,1,...) custom-call(s32[9,16]{1,0:T(8,128)S(1)} %concatenate.12.info, ...), custom_call_target="tpu_custom_call" | custom-call | tf_op jit(solution)/shard_map/pallas_call | solution.py:228
  313.4 1.0 copy-done.3
  315.1 12.5 %all-to-all-start.4 = ((f32[128,16,128]{2,1,0:T(8,128)}), f32[128,16,128]{2,1,0:T(8,128)S(1)}, u32[]{:S(2)}, u32[]{:S(2)}) async-start(f32[128,16,128]{2,1,0:T(8,128)} %bitcast.53), calls=%async_computation.4 | async-start | bytes 2097152 | tf_op jit(solution)/shard_map/all_to_all | solution.py:239
  327.7 1.5 collective-permute-start.20
  329.1 26.7 %all-to-all-done.4 = f32[128,16,128]{2,1,0:T(8,128)S(1)} async-done(((f32[128,16,128]{2,1,0:T(8,128)}), f32[128,16,128]{2,1,0:T(8,128)S(1)}, u32[]{:S(2)}, u32[]{:S(2)}) %all-to-all-start.4) | async-done | bytes 1048608 | tf_op jit(solution)/shard_map/all_to_all | solution.py:239
  355.9 1.9 add_bitcast_fusion
  359.3 6.6 %all-to-all-start.5 = ((f32[128,8,128]{2,1,0:T(8,128)}), f32[128,8,128]{2,1,0:T(8,128)S(1)}, u32[]{:S(2)}, u32[]{:S(2)}) async-start(f32[128,8,128]{2,1,0:T(8,128)} %bitcast.56), calls=%async_computation.5 | async-start | bytes 1048576 | tf_op jit(solution)/shard_map/all_to_all | solution.py:239
  365.9 14.2 %all-to-all-done.5 = f32[128,8,128]{2,1,0:T(8,128)S(1)} async-done(((f32[128,8,128]{2,1,0:T(8,128)}), f32[128,8,128]{2,1,0:T(8,128)S(1)}, u32[]{:S(2)}, u32[]{:S(2)}) %all-to-all-start.5) | async-done | bytes 524320 | tf_op jit(solution)/shard_map/all_to_all | solution.py:239
  380.2 1.7 copy-done.1
  381.9 5.7 %shard_map.92 = (f32[2,512,512]{2,1,0:T(8,128)}, f32[2,256,256]{2,1,0:T(8,128)}) custom-call(f32[1024,128]{1,0:T(8,128)S(1)} %bitcast.50, f32[2,768,768]{2,1,0:T(8,128)} %get-tuple-element.78.o, f32[2,768,768]{2,1,0:T(8,128)} %get-tuple-element.68.n, f32[768,768]{1,0:T(8,128)S(1)} %copy-done.1, f32[2,768,256]{2,1,0:T(8,128)S(1)} %collective-permute-done.19.zl, ...), custom_call_target="tpu_custom_call" | custom-call | tf_op jit(solution)/shard_map/pallas_call | solution.py:287
  (59 shorter events, 4.1 us)
Async XLA Ops:
  0.6 7.3 %copy-start.8 = (f32[2,512,512]{2,1,0:T(8,128)S(1)}, f32[2,512,512]{2,1,0:T(8,128)}, u32[]{:S(2)}) copy-start(f32[2,512,512]{2,1,0:T(8,128)} %tile.1) | copy-start | bytes 6291460
  2.1 30.7 %copy-start.13 = (s32[1,1,4,2]{2,3,1,0:T(2,128)S(1)}, s32[1,1,4,2]{2,3,1,0:T(2,128)}, u32[]{:S(2)}) copy-start(s32[1,1,4,2]{2,3,1,0:T(2,128)} %param.10) | copy-start | bytes 100
  2.1 50.2 %copy-start = (f32[1,1,4,256,256]{4,3,2,1,0:T(8,128)S(1)}, f32[1,1,4,256,256]{4,3,2,1,0:T(8,128)}, u32[]{:S(2)}) copy-start(f32[1,1,4,256,256]{4,3,2,1,0:T(8,128)} %param.9) | copy-start | bytes 3145732
  2.1 50.2 %copy-start.2 = (f32[2,256,256]{2,1,0:T(8,128)S(1)}, f32[2,256,256]{2,1,0:T(8,128)}, u32[]{:S(2)}) copy-start(f32[2,256,256]{2,1,0:T(8,128)} %probe.1) | copy-start | bytes 1572868
  2.1 27.7 %collective-permute-start.4 = (f32[2,256,512]{2,1,0:T(8,128)S(1)}, f32[2,256,512]{2,1,0:T(8,128)S(1)}, u32[]{:S(2)}, u32[]{:S(2)}) collective-permute-start(f32[2,256,512]{2,1,0:T(8,128)S(1)} %slice.71), channel_id=1, source_target_pairs={{8,0},{16,8},{24,16},{32,24},{40,32},{48,40},{56,48},{64,56},{72,6... | collective-permute-start | bytes 3145736 | tf_op jit(solution)/shard_map/ppermute | solution.py:29
  9.0 43.3 %collective-permute-start.5 = (f32[2,512,256]{2,1,0:T(8,128)}, f32[2,512,256]{2,1,0:T(8,128)}, u32[]{:S(2)}, u32[]{:S(2)}) collective-permute-start(f32[2,512,256]{2,1,0:T(8,128)} %slice.72), channel_id=1, source_target_pairs={{1,0},{2,1},{3,2},{4,3},{5,4},{6,5},{7,6},{0,7},{9,8},{10,9},{11,1... | collective-permute-start | bytes 3145736 | tf_op jit(solution)/shard_map/ppermute | solution.py:29
  30.6 21.7 %collective-permute-start.6 = (f32[2,256,256]{2,1,0:T(8,128)}, f32[2,256,256]{2,1,0:T(8,128)S(1)}, u32[]{:S(2)}, u32[]{:S(2)}) collective-permute-start(f32[2,256,256]{2,1,0:T(8,128)} %slice.92), channel_id=1, source_target_pairs={{1,0},{2,1},{3,2},{4,3},{5,4},{6,5},{7,6},{0,7},{9,8},{10,9},{11,1... | collective-permute-start | bytes 1572872 | tf_op jit(solution)/shard_map/ppermute | solution.py:29
  32.9 7.9 %collective-permute-start.1 = (s32[1,16]{1,0:T(1,128)S(1)}, s32[1,16]{1,0:T(1,128)S(1)}, u32[]{:S(2)}, u32[]{:S(2)}) collective-permute-start(s32[1,16]{1,0:T(1,128)S(1)} %add_bitcast_fusion.5), channel_id=1, source_target_pairs={{1,0},{2,1},{3,2},{4,3},{5,4},{6,5},{7,6},{0,7},{9,8},{10,9},{11,1... | collective-permute-start | bytes 200 | tf_op jit(solution)/shard_map/ppermute | solution.py:29
  35.5 5.3 %collective-permute-start = (s32[1,16]{1,0:T(1,128)S(1)}, s32[1,16]{1,0:T(1,128)S(1)}, u32[]{:S(2)}, u32[]{:S(2)}) collective-permute-start(s32[1,16]{1,0:T(1,128)S(1)} %add_bitcast_fusion.5), channel_id=1, source_target_pairs={{7,0},{0,1},{1,2},{2,3},{3,4},{4,5},{5,6},{6,7},{15,8},{8,9},{9,10... | collective-permute-start | bytes 200 | tf_op jit(solution)/shard_map/ppermute | solution.py:29
  40.9 6.3 %collective-permute-start.3 = (s32[3,16]{1,0:T(4,128)S(1)}, s32[3,16]{1,0:T(4,128)S(1)}, u32[]{:S(2)}, u32[]{:S(2)}) collective-permute-start(s32[3,16]{1,0:T(4,128)S(1)} %pad_add_fusion), channel_id=1, source_target_pairs={{8,0},{16,8},{24,16},{32,24},{40,32},{48,40},{56,48},{64,56},{72,6... | collective-permute-start | bytes 584 | tf_op jit(solution)/shard_map/ppermute | solution.py:29
  46.5 5.8 %collective-permute-start.2 = (s32[3,16]{1,0:T(4,128)S(1)}, s32[3,16]{1,0:T(4,128)S(1)}, u32[]{:S(2)}, u32[]{:S(2)}) collective-permute-start(s32[3,16]{1,0:T(4,128)S(1)} %pad_add_fusion), channel_id=1, source_target_pairs={{120,0},{0,8},{8,16},{16,24},{24,32},{32,40},{40,48},{48,56},{56,6... | collective-permute-start | bytes 584 | tf_op jit(solution)/shard_map/ppermute | solution.py:29
  72.0 46.8 %copy-start.5 = (f32[2,256,256]{2,1,0:T(8,128)}, f32[2,256,256]{2,1,0:T(8,128)S(1)}, u32[]{:S(2)}) copy-start(f32[2,256,256]{2,1,0:T(8,128)S(1)} %get-tuple-element.45) | copy-start | bytes 1572868
  72.0 46.8 %copy-start.6 = (f32[2,256,256]{2,1,0:T(8,128)}, f32[2,256,256]{2,1,0:T(8,128)S(1)}, u32[]{:S(2)}) copy-start(f32[2,256,256]{2,1,0:T(8,128)S(1)} %get-tuple-element.44) | copy-start | bytes 1572868
  72.0 42.7 %collective-permute-start.7 = (f32[2,768,256]{2,1,0:T(8,128)}, f32[2,768,256]{2,1,0:T(8,128)S(1)}, u32[]{:S(2)}, u32[]{:S(2)}) collective-permute-start(f32[2,768,256]{2,1,0:T(8,128)} %get-tuple-element.43), channel_id=1, source_target_pairs={{7,0},{0,1},{1,2},{2,3},{3,4},{4,5},{5,6},{6,7},{15,8},{8,9},{9,10... | collective-permute-start | bytes 4718600 | tf_op jit(solution)/shard_map/ppermute | solution.py:29
  72.0 42.7 %collective-permute-start.8 = (f32[2,768,256]{2,1,0:T(8,128)}, f32[2,768,256]{2,1,0:T(8,128)S(1)}, u32[]{:S(2)}, u32[]{:S(2)}) collective-permute-start(f32[2,768,256]{2,1,0:T(8,128)} %get-tuple-element.42), channel_id=1, source_target_pairs={{1,0},{2,1},{3,2},{4,3},{5,4},{6,5},{7,6},{0,7},{9,8},{10,9},{11,1... | collective-permute-start | bytes 4718600 | tf_op jit(solution)/shard_map/ppermute | solution.py:29
  114.7 3.0 copy-start.9
  114.7 3.0 copy-start.10
  118.8 50.7 %collective-permute-start.11 = (f32[2,2,256,256]{3,2,1,0:T(8,128)}, f32[2,2,256,256]{3,2,1,0:T(8,128)}, u32[]{:S(2)}, u32[]{:S(2)}) collective-permute-start(f32[2,2,256,256]{3,2,1,0:T(8,128)} %pad_maximum_fusion), channel_id=1, source_target_pairs={{8,0},{16,8},{24,16},{32,24},{40,32},{48,40},{56,48},{64,56},{72,6... | collective-permute-start | bytes 3145736 | tf_op jit(solution)/shard_map/ppermute | solution.py:29
  119.8 49.6 %collective-permute-start.12 = (f32[2,2,256,256]{3,2,1,0:T(8,128)}, f32[2,2,256,256]{3,2,1,0:T(8,128)}, u32[]{:S(2)}, u32[]{:S(2)}) collective-permute-start(f32[2,2,256,256]{3,2,1,0:T(8,128)} %pad_maximum_fusion.1), channel_id=1, source_target_pairs={{120,0},{0,8},{8,16},{16,24},{24,32},{32,40},{40,48},{48,56},{56,6... | collective-permute-start | bytes 3145736 | tf_op jit(solution)/shard_map/ppermute | solution.py:29
  122.3 32.3 %collective-permute-start.9 = (f32[2,256,256]{2,1,0:T(8,128)}, f32[2,256,256]{2,1,0:T(8,128)S(1)}, u32[]{:S(2)}, u32[]{:S(2)}) collective-permute-start(f32[2,256,256]{2,1,0:T(8,128)} %copy-done.6), channel_id=1, source_target_pairs={{8,0},{16,8},{24,16},{32,24},{40,32},{48,40},{56,48},{64,56},{72,6... | collective-permute-start | bytes 1572872 | tf_op jit(solution)/shard_map/ppermute | solution.py:29
  125.7 37.5 %collective-permute-start.10 = (f32[2,256,256]{2,1,0:T(8,128)}, f32[2,256,256]{2,1,0:T(8,128)}, u32[]{:S(2)}, u32[]{:S(2)}) collective-permute-start(f32[2,256,256]{2,1,0:T(8,128)} %copy-done.5), channel_id=1, source_target_pairs={{120,0},{0,8},{8,16},{16,24},{24,32},{32,40},{40,48},{48,56},{56,6... | collective-permute-start | bytes 1572872 | tf_op jit(solution)/shard_map/ppermute | solution.py:29
  127.3 42.1 %all-to-all-start.1 = ((f32[128,8,128]{2,1,0:T(8,128)}), f32[128,8,128]{2,1,0:T(8,128)S(1)}, u32[]{:S(2)}, u32[]{:S(2)}) async-start(f32[128,8,128]{2,1,0:T(8,128)} %bitcast.14), calls=%async_computation.1 | async-start | bytes 1048576 | tf_op jit(solution)/shard_map/all_to_all | solution.py:239
  194.2 40.7 %collective-permute-start.13 = (f32[2,768,256]{2,1,0:T(8,128)}, f32[2,768,256]{2,1,0:T(8,128)S(1)}, u32[]{:S(2)}, u32[]{:S(2)}) collective-permute-start(f32[2,768,256]{2,1,0:T(8,128)} %get-tuple-element.56), channel_id=1, source_target_pairs={{7,0},{0,1},{1,2},{2,3},{3,4},{4,5},{5,6},{6,7},{15,8},{8,9},{9,10... | collective-permute-start | bytes 4718600 | tf_op jit(solution)/shard_map/ppermute | solution.py:29
  194.2 40.7 %collective-permute-start.14 = (f32[2,768,256]{2,1,0:T(8,128)}, f32[2,768,256]{2,1,0:T(8,128)S(1)}, u32[]{:S(2)}, u32[]{:S(2)}) collective-permute-start(f32[2,768,256]{2,1,0:T(8,128)} %get-tuple-element.55), channel_id=1, source_target_pairs={{1,0},{2,1},{3,2},{4,3},{5,4},{6,5},{7,6},{0,7},{9,8},{10,9},{11,1... | collective-permute-start | bytes 4718600 | tf_op jit(solution)/shard_map/ppermute | solution.py:29
  235.0 3.0 copy-start.11
  235.0 3.0 copy-start.12
  239.0 50.2 %collective-permute-start.17 = (f32[2,2,256,256]{3,2,1,0:T(8,128)}, f32[2,2,256,256]{3,2,1,0:T(8,128)S(1)}, u32[]{:S(2)}, u32[]{:S(2)}) collective-permute-start(f32[2,2,256,256]{3,2,1,0:T(8,128)} %pad_maximum_fusion.2), channel_id=1, source_target_pairs={{8,0},{16,8},{24,16},{32,24},{40,32},{48,40},{56,48},{64,56},{72,6... | collective-permute-start | bytes 3145736 | tf_op jit(solution)/shard_map/ppermute | solution.py:29
  240.1 49.1 %collective-permute-start.18 = (f32[2,2,256,256]{3,2,1,0:T(8,128)}, f32[2,2,256,256]{3,2,1,0:T(8,128)}, u32[]{:S(2)}, u32[]{:S(2)}) collective-permute-start(f32[2,2,256,256]{3,2,1,0:T(8,128)} %pad_maximum_fusion.3), channel_id=1, source_target_pairs={{120,0},{0,8},{8,16},{16,24},{24,32},{32,40},{40,48},{48,56},{56,6... | collective-permute-start | bytes 3145736 | tf_op jit(solution)/shard_map/ppermute | solution.py:29
  241.6 33.3 %collective-permute-start.15 = (f32[2,256,256]{2,1,0:T(8,128)}, f32[2,256,256]{2,1,0:T(8,128)S(1)}, u32[]{:S(2)}, u32[]{:S(2)}) collective-permute-start(f32[2,256,256]{2,1,0:T(8,128)} %get-tuple-element.57), channel_id=1, source_target_pairs={{8,0},{16,8},{24,16},{32,24},{40,32},{48,40},{56,48},{64,56},{72,6... | collective-permute-start | bytes 1572872 | tf_op jit(solution)/shard_map/ppermute | solution.py:29
  244.9 38.4 %collective-permute-start.16 = (f32[2,256,256]{2,1,0:T(8,128)}, f32[2,256,256]{2,1,0:T(8,128)}, u32[]{:S(2)}, u32[]{:S(2)}) collective-permute-start(f32[2,256,256]{2,1,0:T(8,128)} %get-tuple-element.58), channel_id=1, source_target_pairs={{120,0},{0,8},{8,16},{16,24},{24,32},{32,40},{40,48},{48,56},{56,6... | collective-permute-start | bytes 1572872 | tf_op jit(solution)/shard_map/ppermute | solution.py:29
  245.9 43.3 %all-to-all-start.3 = ((f32[128,8,128]{2,1,0:T(8,128)}), f32[128,8,128]{2,1,0:T(8,128)S(1)}, u32[]{:S(2)}, u32[]{:S(2)}) async-start(f32[128,8,128]{2,1,0:T(8,128)} %bitcast.22), calls=%async_computation.3 | async-start | bytes 1048576 | tf_op jit(solution)/shard_map/all_to_all | solution.py:239
  313.3 1.0 copy-start.3
  314.3 0.8 copy-start.7
  315.1 40.7 %collective-permute-start.19 = (f32[2,768,256]{2,1,0:T(8,128)}, f32[2,768,256]{2,1,0:T(8,128)S(1)}, u32[]{:S(2)}, u32[]{:S(2)}) collective-permute-start(f32[2,768,256]{2,1,0:T(8,128)} %get-tuple-element.69), channel_id=1, source_target_pairs={{7,0},{0,1},{1,2},{2,3},{3,4},{4,5},{5,6},{6,7},{15,8},{8,9},{9,10... | collective-permute-start | bytes 4718600 | tf_op jit(solution)/shard_map/ppermute | solution.py:29
  315.1 40.7 %all-to-all-start.4 = ((f32[128,16,128]{2,1,0:T(8,128)}), f32[128,16,128]{2,1,0:T(8,128)S(1)}, u32[]{:S(2)}, u32[]{:S(2)}) async-start(f32[128,16,128]{2,1,0:T(8,128)} %bitcast.53), calls=%async_computation.4 | async-start | bytes 2097152 | tf_op jit(solution)/shard_map/all_to_all | solution.py:239
  327.7 38.2 %collective-permute-start.20 = (f32[2,256,256]{2,1,0:T(8,128)}, f32[2,256,256]{2,1,0:T(8,128)S(1)}, u32[]{:S(2)}, u32[]{:S(2)}) collective-permute-start(f32[2,256,256]{2,1,0:T(8,128)} %copy-done.7), channel_id=1, source_target_pairs={{120,0},{0,8},{8,16},{16,24},{24,32},{32,40},{40,48},{48,56},{56,6... | collective-permute-start | bytes 1572872 | tf_op jit(solution)/shard_map/ppermute | solution.py:29
  357.8 22.4 %collective-permute-start.21 = (f32[1,2,256,256]{3,2,1,0:T(8,128)}, f32[1,2,256,256]{3,2,1,0:T(8,128)}, u32[]{:S(2)}, u32[]{:S(2)}) collective-permute-start(f32[1,2,256,256]{3,2,1,0:T(8,128)} %add_bitcast_fusion), channel_id=1, source_target_pairs={{120,0},{0,8},{8,16},{16,24},{24,32},{32,40},{40,48},{48,56},{56,6... | collective-permute-start | bytes 1572872 | tf_op jit(solution)/shard_map/ppermute | solution.py:29
  358.5 0.8 copy-start.4
  359.3 20.9 %all-to-all-start.5 = ((f32[128,8,128]{2,1,0:T(8,128)}), f32[128,8,128]{2,1,0:T(8,128)S(1)}, u32[]{:S(2)}, u32[]{:S(2)}) async-start(f32[128,8,128]{2,1,0:T(8,128)} %bitcast.56), calls=%async_computation.5 | async-start | bytes 1048576 | tf_op jit(solution)/shard_map/all_to_all | solution.py:239
  380.2 1.7 copy-start.1

commit v2 on v1

v2 whole, which is shorter than its diff:
```python
import math

import jax
import jax.numpy as jnp
import numpy as np
from jax import lax
from jax.experimental import pallas as pl
from jax.experimental.pallas import tpu as pltpu
from jax.sharding import PartitionSpec as P

PASSES = 3
F = 256
TILE = 512
WIDE = TILE + F
HALF = F // 2
LANES = 128
FRAMES_LIMIT = 18

amp_floor = 0.1
object_damping = 0.5
probe_damping = 1.0

VMEM = pl.BlockSpec(memory_space=pltpu.VMEM)
SMEM = pl.BlockSpec(memory_space=pltpu.SMEM)


def passed_along(block, axis, distance):
    size = lax.axis_size(axis)
    route = [((i - distance) % size, i) for i in range(size)]
    return lax.ppermute(block, axis, route)


def split(x):
    high = x.astype(jnp.bfloat16)
    low = (x - high.astype(jnp.float32)).astype(jnp.bfloat16)
    return high, low


def tables():
    k = np.arange(F)
    angles = (k[:, None] * k[None, :] % F) * (-2.0 * math.pi / F)
    re = np.cos(angles) / math.sqrt(F)
    im = np.sin(angles) / math.sqrt(F)
    left = np.block([[re, -im], [im, re]]).astype(np.float32)
    right = np.block([[re, im], [-im, re]]).astype(np.float32)

    def terms(m):
        high = m.astype(jnp.bfloat16)
        low = (m - high.astype(np.float32)).astype(jnp.bfloat16)
        return high, low

    lh, ll = terms(left)
    rh, rl = terms(right)
    return np.concatenate([lh, lh, ll], 1), np.concatenate([rh, rh, rl], 0)


def stacked(re, im):
    h, l = split(jnp.concatenate([re, im], 0))
    return jnp.concatenate([h, l, h], 0)


def abreast(y):
    h, l = split(jnp.concatenate([y[:F], y[F:]], 1))
    return jnp.concatenate([h, l, h], 1)


def transforms(fields, left, right):
    ys = [jnp.dot(left[...], stacked(re, im), preferred_element_type=jnp.float32) for re, im in fields]
    zs = [jnp.dot(abreast(y), right[...], preferred_element_type=jnp.float32) for y in ys]
    return [(z[:, :F], z[:, F:]) for z in zs]


def window(ref, lead, r, c):
    r0 = pl.multiple_of((r // 8) * 8, 8)
    c0 = pl.multiple_of((c // LANES) * LANES, LANES)
    rs, cs = r - r0, c - c0
    w = ref[lead + (pl.ds(r0, F + 8), pl.ds(c0, F + LANES))]
    lane = lax.broadcasted_iota(jnp.int32, (F + 8, LANES), 1)
    back = lax.rem(LANES - cs, LANES)
    t = [pltpu.roll(w[:, i * LANES : (i + 1) * LANES], back, 1) for i in range(3)]
    w = jnp.concatenate([jnp.where(lane < LANES - cs, t[i], t[i + 1]) for i in range(2)], 1)
    w = pltpu.roll(w.reshape(F // 8 + 1, 8, F), lax.rem(8 - rs, 8), 1)
    sub = lax.broadcasted_iota(jnp.int32, (F // 8, 8, F), 1)
    return jnp.where(sub < 8 - rs, w[:-1], w[1:]).reshape(F, F)


def deposit(ref, lead, r, c, x):
    r0 = pl.multiple_of((r // 8) * 8, 8)
    c0 = pl.multiple_of((c // LANES) * LANES, LANES)
    rs, cs = r - r0, c - c0
    w = pltpu.roll(x.reshape(F // 8, 8, F), rs, 1)
    zero = jnp.zeros((1, 8, F), jnp.float32)
    sub = lax.broadcasted_iota(jnp.int32, (F // 8 + 1, 8, F), 1)
    w = jnp.where(sub >= rs, jnp.concatenate([w, zero], 0), jnp.concatenate([zero, w], 0))
    w = w.reshape(F + 8, F)
    lane = lax.broadcasted_iota(jnp.int32, (F + 8, LANES), 1)
    a = pltpu.roll(w[:, :LANES], cs, 1)
    b = pltpu.roll(w[:, LANES:], cs, 1)
    t = [jnp.where(lane >= cs, a, 0.0), jnp.where(lane >= cs, b, a), jnp.where(lane >= cs, 0.0, b)]
    at = lead + (pl.ds(r0, F + 8), pl.ds(c0, F + LANES))
    ref[at] = ref[at] + jnp.concatenate(t, 1)


def visit_frames(info, amplitude, left, right, ob, pr, canvas, grads):
    canvas[...] = jnp.zeros_like(canvas)
    grads[...] = jnp.zeros_like(grads)
    count = info[4, 8]

    def pair(i, carry):
        slots = (2 * i, 2 * i + 1)
        live = (1.0, (2 * i + 1 < count).astype(jnp.float32))
        at = [(info[4, k], info[4, 4 + k]) for k in slots]
        patches = [[window(ob, (p,), r, c) for p in range(2)] for r, c in at]
        qr, qi = pr[0], pr[1]
        waves = [(qr * fr - qi * fi, qr * fi + qi * fr) for fr, fi in patches]
        turned = []
        for k, w, (zr, zi) in zip(slots, live, transforms(waves, left, right)):
            power = zr * zr + zi * zi
            ratio = (amplitude[k] * lax.rsqrt(jnp.maximum(power, amp_floor * amp_floor)) - 1.0) * w
            turned.append((zr * ratio, -(zi * ratio)))
        for w, (r, c), (fr, fi), (br, bi) in zip(live, at, patches, transforms(turned, left, right)):
            grads[0] += fr * br - fi * bi
            grads[1] -= fr * bi + fi * br
            grads[2] += (fr * fr + fi * fi) * w
            deposit(canvas, (0,), r, c, qr * br - qi * bi)
            deposit(canvas, (1,), r, c, -(qr * bi) - qi * br)
        return carry

    lax.fori_loop(0, (count + 1) // 2, pair, 0)


def hand_out(canvas, pr, zl_out, zr_out, up_out, mid_out, dn_out, p_out):
    zl_out[...] = canvas[:, :, :F]
    zr_out[...] = canvas[:, :, TILE:]
    up_out[:2] = canvas[:, :F, F:TILE]
    mid_out[...] = canvas[:, F:TILE, F:TILE]
    dn_out[:2] = canvas[:, TILE:, F:TILE]
    p_out[...] = pr[...]


def pack_kernel(grads, g_out):
    for p in range(3):
        for h in range(2):
            for t in range(2):
                g_out[pl.ds(4 * p + 2 * t + h, HALF, stride=12), :] = grads[p, h * HALF : (h + 1) * HALF, t * LANES : (t + 1) * LANES]


def first_kernel(info, amp, left, right, probe, tile, below, beside, corner, *rest):
    ob, grads, outs, (pr, canvas) = rest[0], rest[1], rest[2:8], rest[8:]
    ob[:, :TILE, :TILE] = tile[...]
    ob[:, TILE:, :TILE] = below[...]
    ob[:, :TILE, TILE:] = beside[...]
    ob[:, TILE:, TILE:] = corner[...]
    pr[...] = probe[...]
    visit_frames(info, amp, left, right, ob, pr, canvas, grads)
    hand_out(canvas, pr, *outs)


def gathered_probe(pg, pr):
    for p in range(2):
        for h in range(2):
            for t in range(2):
                pr[p, h * HALF : (h + 1) * HALF, t * LANES : (t + 1) * LANES] = pg[pl.ds(4 * p + 2 * t + h, HALF, stride=8), :]


def refreshed(put, size, o, l, zl, zr, up, mid, dn, left_in, right_in, cup, cdn, sup, sdn):
    for i in range(size // F):
        for j in range(size // F):
            rows, cols = slice(i * F, (i + 1) * F), slice(j * F, (j + 1) * F)
            scale = 1.0 / (l[rows, cols] + object_damping)
            for p in range(2):
                if j == 0:
                    s = zl[p, rows, :] + left_in[p, rows, :]
                elif j == 1:
                    s = (up, mid, dn)[i][p]
                else:
                    s = zr[p, rows, :] + right_in[p, rows, :]
                if i == 0:
                    s = s + (cdn[p] if j == 1 else sdn[j // 2, p])
                if i == 2:
                    s = s + (cup[p] if j == 1 else sup[j // 2, p])
                put(p, rows, cols, o[p, rows, cols] + s * scale)


def next_kernel(info, amp, left, right, pg, o, l, zl, zr, up, mid, dn, left_in, right_in, cup, cdn, sup, sdn, *rest):
    ob, grads, outs, (pr, canvas) = rest[0], rest[1], rest[2:8], rest[8:]

    def put(p, rows, cols, value):
        ob[p, rows, cols] = value

    refreshed(put, WIDE, o, l, zl, zr, up, mid, dn, left_in, right_in, cup, cdn, sup, sdn)
    gathered_probe(pg, pr)
    visit_frames(info, amp, left, right, ob, pr, canvas, grads)
    hand_out(canvas, pr, *outs)


def last_kernel(pg, o, l, zl, up, mid, left_in, cdn, sdn, o_out, p_out):
    def put(p, rows, cols, value):
        o_out[p, rows, cols] = value

    refreshed(put, TILE, o, l, zl, None, up, mid, None, left_in, None, None, cdn, None, sdn)
    gathered_probe(pg, p_out)


def glow_kernel(info, pr, out, glow):
    glow[F : F + WIDE, F : F + WIDE] = jnp.zeros((WIDE, WIDE), jnp.float32)

    def near(i, carry):
        n, k = i // 4, lax.rem(i, 4)
        r = info[n, k] + TILE * (n // 3) - (TILE - F)
        c = info[n, 4 + k] + TILE * lax.rem(n, 3) - (TILE - F)
        live = k < info[n, 8]
        meets = (r > 0) & (r < F + WIDE) & (c > 0) & (c < F + WIDE)

        @pl.when(live & meets)
        def _():
            deposit(glow, (), r, c, pr[0] * pr[0] + pr[1] * pr[1])

        return carry

    lax.fori_loop(0, 36, near, 0)
    out[...] = glow[F : F + WIDE, F : F + WIDE]


def middle_kernel(last, g, old, zl, left_in, *rest):
    if last:
        sdn, new, spread = rest
        sdn[0] = zl[:, TILE:] + left_in[:, TILE:]
    else:
        zr, right_in, sup, sdn, new, spread = rest
        sup[0] = zl[:, :F] + left_in[:, :F]
        sup[1] = zr[:, :F] + right_in[:, :F]
        sdn[0] = zl[:, TILE:] + left_in[:, TILE:]
        sdn[1] = zr[:, TILE:] + right_in[:, TILE:]
    s = jnp.sum(g[...].reshape(HALF // 2, 24, LANES), axis=0)
    s = s[:12] + s[12:]
    value = old[...] + s[:8] / (jnp.concatenate([s[8:], s[8:]], 0) + probe_damping)
    new[...] = value
    spread[...] = jnp.broadcast_to(value[None], (HALF, 8, LANES)).reshape(HALF * 8, LANES)


def f32(*shape):
    return jax.ShapeDtypeStruct(shape, jnp.float32)


def call(kernel, args, outs, scratch=(), limit=14, smem=(), cost=None, alias=None):
    return pl.pallas_call(
        kernel,
        out_shape=tuple(outs),
        in_specs=[SMEM if i in smem else VMEM for i in range(len(args))],
        out_specs=tuple(VMEM for _ in outs),
        scratch_shapes=list(scratch),
        compiler_params=pltpu.CompilerParams(vmem_limit_bytes=limit << 20),
        cost_estimate=cost,
        input_output_aliases=alias or {},
    )(*args)


def call_frames(kernel, *args, alias=None):
    scratch = [
        pltpu.VMEM((2, F, F), jnp.float32),
        pltpu.VMEM((2, WIDE, WIDE), jnp.float32),
    ]
    outs = (
        f32(2, WIDE, WIDE), f32(3, F, F), f32(2, WIDE, F), f32(2, WIDE, F),
        f32(3, F, F), f32(2, F, F), f32(3, F, F), f32(2, F, F),
    )
    return call(kernel, args, outs, scratch, limit=FRAMES_LIMIT, smem=(0,), alias=alias)


def glow_of(info, pr):
    return call(
        glow_kernel, (info, pr), (f32(WIDE, WIDE),), [pltpu.VMEM((WIDE + 2 * F, WIDE + 2 * F), jnp.float32)],
        limit=8, smem=(0,), cost=pl.CostEstimate(flops=10 << 20, bytes_accessed=12 << 20, transcendentals=0),
    )[0]


def everyone(x):
    return lax.all_to_all(x, ("row", "col"), 0, 0)


def shards(object_field, probe, amplitude, positions, counts):
    me = lax.axis_index(("row", "col"))
    left, right = (jnp.asarray(t) for t in tables())
    amp = amplitude[0, 0]
    mine = jnp.concatenate([positions[0, 0, :, 0], positions[0, 0, :, 1], counts[0], jnp.zeros((7,), jnp.int32)])[None]

    below = passed_along(object_field[:, :F, :], "row", -1)
    beside = passed_along(object_field[:, :, :F], "col", -1)
    info = jnp.concatenate([passed_along(mine, "col", 1), mine, passed_along(mine, "col", -1)], 0)
    info = jnp.concatenate([passed_along(info, "row", 1), info, passed_along(info, "row", -1)], 0)
    below, info = lax.optimization_barrier((below, info))
    corner = passed_along(below[:, :, :F], "col", -1)
    light = glow_of(info, probe)

    own = lax.dynamic_slice(probe.reshape(2, 2, HALF, 2, LANES), (0, 0, me, 0, 0), (2, 2, 1, 2, LANES))
    own = own[:, :, 0].transpose(0, 2, 1, 3).reshape(8, LANES)
    own, light, corner = lax.optimization_barrier((own, light, corner))

    state = call_frames(first_kernel, info, amp, left, right, probe, object_field, below, beside, corner)
    for sweep in range(PASSES):
        last = sweep == PASSES - 1
        ob, grad, to_left, to_right, up, mid, down, pr = state
        grad = call(pack_kernel, (grad,), (f32(HALF * 12, LANES),))[0].reshape(HALF, 3, 4, LANES)
        from_left = passed_along(to_right, "col", 1)
        centre_down = passed_along(down, "row", 1)
        moved = [from_left, centre_down]
        if not last:
            moved += [passed_along(to_left, "col", -1), passed_along(up, "row", -1)]
        grad, to_left, to_right = lax.optimization_barrier((grad, to_left, to_right))
        grad = everyone(grad)
        grad, moved = lax.optimization_barrier((grad, moved))
        grad = grad.reshape(HALF * 12, LANES)
        tail = (f32(8, LANES), f32(HALF * 8, LANES))
        if last:
            from_left, centre_down = moved
            side_down, own, spread = call(
                lambda *refs: middle_kernel(True, *refs), (grad, own, to_left, from_left), (f32(1, 2, F, F),) + tail,
            )
            sides = (side_down,)
            moved = (passed_along(side_down, "row", 1),)
        else:
            from_left, centre_down, from_right, centre_up = moved
            side_up, side_down, own, spread = call(
                lambda *refs: middle_kernel(False, *refs), (grad, own, to_left, from_left, to_right, from_right),
                (f32(2, 2, F, F), f32(2, 2, F, F)) + tail,
            )
            sides = (side_up, side_down)
            moved = (passed_along(side_up, "row", -1), passed_along(side_down, "row", 1))
        sides, spread = lax.optimization_barrier((sides, spread))
        pg = everyone(spread.reshape(HALF, 2, 4, LANES)).reshape(HALF * 8, LANES)
        pg, pr = lax.optimization_barrier((pg, pr))
        if sweep > 0:
            light = glow_of(info, pr)
        if last:
            return call(
                last_kernel, (pg, ob, light, to_left, up, mid, from_left, centre_down, moved[0]),
                (f32(2, TILE, TILE), f32(2, F, F)),
            )
        state = call_frames(
            next_kernel, info, amp, left, right, pg, ob, light, to_left, to_right, up, mid, down,
            from_left, from_right, centre_up, centre_down, moved[0], moved[1], alias={5: 0},
        )


def solution(mesh):
    return jax.shard_map(
        shards,
        mesh=mesh,
        in_specs=(
            P(None, "row", "col"),
            P(),
            P("row", "col", None, None, None),
            P("row", "col", None, None),
            P("row", "col"),
        ),
        out_specs=(P(None, "row", "col"), P()),
        check_vma=False,
    )
```

time: 387 us -> 298 us (0.77)
  waiting for transfers between devices: 137 us -> 15.6 us
  blocking collectives: 64 us -> 181 us
  starting transfers between devices: 86.4 us -> 37 us
  Pallas kernels: 76.9 us -> 51.3 us
  other arithmetic: 12.2 us -> 0.09 us
    all_to_all x2 -> x6, blocking collectives: 64 us -> 181 us  [everyone(): return lax.all_to_all(x, ('row', 'col'), 0, 0)]
    ppermute x22, waiting for transfers between devices: 84 us -> 15.6 us  [passed_along(): return lax.ppermute(block, axis, route)]
    all_to_all x4 -> x0, waiting for transfers between devices: 53.1 us -> none  [everyone(): return lax.all_to_all(x, ('row', 'col'), 0, 0)]
    all_to_all x4 -> x0, starting transfers between devices: 39.4 us -> none  [everyone(): return lax.all_to_all(x, ('row', 'col'), 0, 0)]
    pallas_call x7 -> x13, Pallas kernels: 76.9 us -> 51.3 us  [call(): pl.pallas_call(kernel, out_shape=tuple(outs), in_specs=[SMEM if i in smem...]
    another operation x6 -> x0, other arithmetic: 10.2 us -> none  [the longest x4 8.11 us: shards(): jnp.stack([numer[:, TILE:, :F] + from_left[:, TILE:], numer[:, TILE:, TIL...]
    ppermute x22, starting transfers between devices: 47 us -> 37 us  [passed_along(): return lax.ppermute(block, axis, route)]
  transfers between devices with their start and end apart: 26 -> 22, of which waited for: 12 -> 4; matrix products, arithmetic and copies ran while one was open for 2% -> 1% of each run, Pallas kernels for 1% -> 3%
where the time goes in v2:
time: 298 us; the launch traced here: 297 us
  blocking collectives  181 us (61%)
  Pallas kernels  51.3 us (17%)
  starting transfers between devices  37 us (12%)
  waiting for transfers between devices  15.6 us (5%)
  local copies, waits for them, and re-layouts  10.5 us (4%)
    all_to_all x6, blocking collectives, everyone(): return lax.all_to_all(x, ('row', 'col'), 0, 0)  181 us
    pallas_call x13, Pallas kernels, call(): pl.pallas_call(kernel, out_shape=tuple(outs), in_specs=[SMEM if i in smem...  51.3 us
    ppermute x22, starting transfers between devices, passed_along(): return lax.ppermute(block, axis, route)  37 us
    ppermute x22, waiting for transfers between devices, passed_along(): return lax.ppermute(block, axis, route)  15.6 us
  transfers between devices with their start and end apart: 22, of which 4 were waited for; matrix products, arithmetic and copies ran while one was open for 1% of the time, Pallas kernels for 3%

profile of v2, /device:TPU:1, one launch (start us, length us, event | category | flops | bytes accessed | tf_op | source)
XLA Modules:
  0.0 297.4 jit_solution(13418911471810868834)
XLA Ops:
  0.6 1.4 slice.15
  2.1 5.8 %collective-permute-start = (f32[2,256,512]{2,1,0:T(8,128)S(1)}, f32[2,256,512]{2,1,0:T(8,128)S(1)}, u32[]{:S(2)}, u32[]{:S(2)}) collective-permute-start(f32[2,256,512]{2,1,0:T(8,128)S(1)} %slice.15), channel_id=1, source_target_pairs={{8,0},{16,8},{24,16},{32,24},{40,32},{48,40},{56,48},{64,56},{72,6... | collective-permute-start | bytes 3145736 | tf_op jit(solution)/shard_map/ppermute | solution.py:30
  7.9 1.1 slice.18
  9.0 1.0 collective-permute-start.5
  10.7 0.1 add_bitcast_fusion
  10.7 3.2 %collective-permute-start.2 = (s32[1,16]{1,0:T(1,128)S(1)}, s32[1,16]{1,0:T(1,128)S(1)}, u32[]{:S(2)}, u32[]{:S(2)}) collective-permute-start(s32[1,16]{1,0:T(1,128)S(1)} %add_bitcast_fusion), channel_id=1, source_target_pairs={{1,0},{2,1},{3,2},{4,3},{5,4},{6,5},{7,6},{0,7},{9,8},{10,9},{11,1... | collective-permute-start | bytes 200 | tf_op jit(solution)/shard_map/ppermute | solution.py:30
  13.9 10.5 %collective-permute-done.2 = s32[1,16]{1,0:T(1,128)S(1)} collective-permute-done((s32[1,16]{1,0:T(1,128)S(1)}, s32[1,16]{1,0:T(1,128)S(1)}, u32[]{:S(2)}, u32[]{:S(2)}) %collective-permute-start.2) | collective-permute-done | bytes 96 | tf_op jit(solution)/shard_map/ppermute | solution.py:30
  24.5 0.6 collective-permute-start.4
  25.1 0.9 collective-permute-start.3
  26.0 3.8 %collective-permute-done.4 = s32[3,16]{1,0:T(4,128)S(1)} collective-permute-done((s32[3,16]{1,0:T(4,128)S(1)}, s32[3,16]{1,0:T(4,128)S(1)}, u32[]{:S(2)}, u32[]{:S(2)}) %collective-permute-start.4) | collective-permute-done | bytes 224 | tf_op jit(solution)/shard_map/ppermute | solution.py:30
  29.8 1.1 collective-permute-done.3
  30.9 0.1 concatenate.12.info
  31.0 0.9 slice.19
  31.9 2.8 collective-permute-start.6
  34.7 1.0 reshape.46
  35.7 0.8 constant_dynamic-slice_fusion
  36.5 1.0 copy-done.7
  37.5 3.4 %shard_map.86.l = f32[768,768]{1,0:T(8,128)S(1)} custom-call(s32[9,16]{1,0:T(8,128)S(1)} %concatenate.12.info, f32[2,256,256]{2,1,0:T(8,128)S(1)} %copy-done.7), custom_call_target="tpu_custom_call" | custom-call | flops 10485760 | bytes 12582912 | tf_op jit(solution)/shard_map/pallas_call | solution.py:247
  40.9 0.1 collective-permute-done.6.corner
  41.1 1.2 copy-done.2
  42.3 1.6 copy-done.5
  43.9 1.2 copy-done.9
  45.1 12.2 %shard_map.87 = (f32[2,768,768]{2,1,0:T(8,128)S(1)}, f32[3,256,256]{2,1,0:T(8,128)S(1)}, f32[2,768,256]{2,1,0:T(8,128)S(1)}, f32[2,768,256]{2,1,0:T(8,128)S(1)},...) custom-call(s32[9,16]{1,0:T(8,128)S(1)} %concatenate.12.info, ...), custom_call_target="tpu_custom_call" | custom-call | tf_op jit(solution)/shard_map/pallas_call | solution.py:247
  57.3 1.7 collective-permute-start.7
  59.1 4.8 %collective-permute-start.10 = (f32[3,256,256]{2,1,0:T(8,128)S(1)}, f32[3,256,256]{2,1,0:T(8,128)S(1)}, u32[]{:S(2)}, u32[]{:S(2)}) collective-permute-start(f32[3,256,256]{2,1,0:T(8,128)S(1)} %get-tuple-element.76.up), channel_id=1, source_target_pairs={{8,0},{16,8},{24,16},{32,24},{40,32},{48,40},{56,48},{64,56},{72,6... | collective-permute-start | bytes 2359304 | tf_op jit(solution)/shard_map/ppermute | solution.py:30
  63.9 0.1 shard_map.88
  63.9 26.5 %all_to_all.30 = f32[128,3,4,128]{3,2,1,0:T(4,128)S(1)} all-to-all(f32[128,3,4,128]{3,2,1,0:T(4,128)S(1)} %bitcast.31), channel_id=1, replica_groups=mesh['row'=16,'col'=8] {'row','col'}, dimensions={0} | all-to-all | bytes 1572864 | tf_op jit(solution)/shard_map/all_to_all | solution.py:279
  90.5 0.3 shard_map.89
  90.9 5.7 %collective-permute-start.11 = (f32[2,2,256,256]{3,2,1,0:T(8,128)S(1)}, f32[2,2,256,256]{3,2,1,0:T(8,128)S(1)}, u32[]{:S(2)}, u32[]{:S(2)}) collective-permute-start(f32[2,2,256,256]{3,2,1,0:T(8,128)S(1)} %get-tuple-element.83), channel_id=1, source_target_pairs={{8,0},{16,8},{24,16},{32,24},{40,32},{48,40},{56,48},{64,56},{72,6... | collective-permute-start | bytes 3145736 | tf_op jit(solution)/shard_map/ppermute | solution.py:30
  96.6 35.3 %all_to_all.31 = f32[128,2,4,128]{3,2,1,0:T(4,128)S(1)} all-to-all(f32[128,2,4,128]{3,2,1,0:T(4,128)S(1)} %bitcast.38), channel_id=1, replica_groups=mesh['row'=16,'col'=8] {'row','col'}, dimensions={0} | all-to-all | bytes 1048576 | tf_op jit(solution)/shard_map/all_to_all | solution.py:279
  131.8 12.7 %shard_map.90 = (f32[2,768,768]{2,1,0:T(8,128)S(1)}, f32[3,256,256]{2,1,0:T(8,128)S(1)}, f32[2,768,256]{2,1,0:T(8,128)S(1)}, f32[2,768,256]{2,1,0:T(8,128)S(1)},...) custom-call(s32[9,16]{1,0:T(8,128)S(1)} %concatenate.12.info, ...), custom_call_target="tpu_custom_call", output_to_operand_aliasing={{0}: (5, {})} | custom-call | tf_op jit(solution)/shard_map/pallas_call | solution.py:247
  144.5 0.0 collective-permute-start.15
  144.6 1.7 collective-permute-start.13
  146.3 4.8 %collective-permute-start.16 = (f32[3,256,256]{2,1,0:T(8,128)S(1)}, f32[3,256,256]{2,1,0:T(8,128)S(1)}, u32[]{:S(2)}, u32[]{:S(2)}) collective-permute-start(f32[3,256,256]{2,1,0:T(8,128)S(1)} %get-tuple-element.97.up), channel_id=1, source_target_pairs={{8,0},{16,8},{24,16},{32,24},{40,32},{48,40},{56,48},{64,56},{72,6... | collective-permute-start | bytes 2359304 | tf_op jit(solution)/shard_map/ppermute | solution.py:30
  151.1 0.1 shard_map.91
  151.2 26.0 %all_to_all.32 = f32[128,3,4,128]{3,2,1,0:T(4,128)S(1)} all-to-all(f32[128,3,4,128]{3,2,1,0:T(4,128)S(1)} %bitcast.32), channel_id=1, replica_groups=mesh['row'=16,'col'=8] {'row','col'}, dimensions={0} | all-to-all | bytes 1572864 | tf_op jit(solution)/shard_map/all_to_all | solution.py:279
  177.2 0.3 shard_map.92
  177.5 3.9 %collective-permute-start.17 = (f32[2,2,256,256]{3,2,1,0:T(8,128)S(1)}, f32[2,2,256,256]{3,2,1,0:T(8,128)S(1)}, u32[]{:S(2)}, u32[]{:S(2)}) collective-permute-start(f32[2,2,256,256]{3,2,1,0:T(8,128)S(1)} %get-tuple-element.104), channel_id=1, source_target_pairs={{8,0},{16,8},{24,16},{32,24},{40,32},{48,40},{56,48},{64,56},{72,6... | collective-permute-start | bytes 3145736 | tf_op jit(solution)/shard_map/ppermute | solution.py:30
  181.4 37.5 %all_to_all.33 = f32[128,2,4,128]{3,2,1,0:T(4,128)S(1)} all-to-all(f32[128,2,4,128]{3,2,1,0:T(4,128)S(1)} %bitcast.39), channel_id=1, replica_groups=mesh['row'=16,'col'=8] {'row','col'}, dimensions={0} | all-to-all | bytes 1048576 | tf_op jit(solution)/shard_map/all_to_all | solution.py:279
  218.9 3.4 %shard_map.93.l = f32[768,768]{1,0:T(8,128)S(1)} custom-call(s32[9,16]{1,0:T(8,128)S(1)} %concatenate.12.info, f32[2,256,256]{2,1,0:T(8,128)S(1)} %get-tuple-element.111.pr), custom_call_target="tpu_custom_call" | custom-call | flops 10485760 | bytes 12582912 | tf_op jit(solution)/shard_map/pallas_call | solution.py:247
  222.3 12.7 %shard_map.94 = (f32[2,768,768]{2,1,0:T(8,128)S(1)}, f32[3,256,256]{2,1,0:T(8,128)S(1)}, f32[2,768,256]{2,1,0:T(8,128)S(1)}, f32[2,768,256]{2,1,0:T(8,128)S(1)},...) custom-call(s32[9,16]{1,0:T(8,128)S(1)} %concatenate.12.info, ...), custom_call_target="tpu_custom_call", output_to_operand_aliasing={{0}: (5, {})} | custom-call | tf_op jit(solution)/shard_map/pallas_call | solution.py:247
  235.0 0.1 collective-permute-start.20
  235.1 0.1 shard_map.95
  235.2 31.6 %all_to_all.34 = f32[128,3,4,128]{3,2,1,0:T(4,128)S(1)} all-to-all(f32[128,3,4,128]{3,2,1,0:T(4,128)S(1)} %bitcast.33), channel_id=1, replica_groups=mesh['row'=16,'col'=8] {'row','col'}, dimensions={0} | all-to-all | bytes 1572864 | tf_op jit(solution)/shard_map/all_to_all | solution.py:279
  266.7 0.7 shard_map.96
  267.4 24.5 %all_to_all.35 = f32[128,2,4,128]{3,2,1,0:T(4,128)S(1)} all-to-all(f32[128,2,4,128]{3,2,1,0:T(4,128)S(1)} %bitcast.40), channel_id=1, replica_groups=mesh['row'=16,'col'=8] {'row','col'}, dimensions={0} | all-to-all | bytes 1048576 | tf_op jit(solution)/shard_map/all_to_all | solution.py:279
  291.9 3.4 %shard_map.97.l = f32[768,768]{1,0:T(8,128)S(1)} custom-call(s32[9,16]{1,0:T(8,128)S(1)} %concatenate.12.info, f32[2,256,256]{2,1,0:T(8,128)S(1)} %get-tuple-element.130.pr), custom_call_target="tpu_custom_call" | custom-call | flops 10485760 | bytes 12582912 | tf_op jit(solution)/shard_map/pallas_call | solution.py:247
  295.3 2.1 shard_map.98
  (48 shorter events, 0.2 us)
Async XLA Ops:
  0.6 7.3 %copy-start.4 = (f32[2,512,512]{2,1,0:T(8,128)S(1)}, f32[2,512,512]{2,1,0:T(8,128)}, u32[]{:S(2)}) copy-start(f32[2,512,512]{2,1,0:T(8,128)} %tile.1) | copy-start | bytes 6291460
  2.1 8.5 %copy-start.10 = (s32[1,1,4,2]{2,3,1,0:T(2,128)S(1)}, s32[1,1,4,2]{2,3,1,0:T(2,128)}, u32[]{:S(2)}) copy-start(s32[1,1,4,2]{2,3,1,0:T(2,128)} %param.10) | copy-start | bytes 100
  2.1 32.6 %copy-start.6 = (f32[2,256,256]{2,1,0:T(8,128)S(1)}, f32[2,256,256]{2,1,0:T(8,128)}, u32[]{:S(2)}) copy-start(f32[2,256,256]{2,1,0:T(8,128)} %probe.1) | copy-start | bytes 1572868
  2.1 28.9 %collective-permute-start = (f32[2,256,512]{2,1,0:T(8,128)S(1)}, f32[2,256,512]{2,1,0:T(8,128)S(1)}, u32[]{:S(2)}, u32[]{:S(2)}) collective-permute-start(f32[2,256,512]{2,1,0:T(8,128)S(1)} %slice.15), channel_id=1, source_target_pairs={{8,0},{16,8},{24,16},{32,24},{40,32},{48,40},{56,48},{64,56},{72,6... | collective-permute-start | bytes 3145736 | tf_op jit(solution)/shard_map/ppermute | solution.py:30
  9.0 32.1 %collective-permute-start.5 = (f32[2,512,256]{2,1,0:T(8,128)}, f32[2,512,256]{2,1,0:T(8,128)}, u32[]{:S(2)}, u32[]{:S(2)}) collective-permute-start(f32[2,512,256]{2,1,0:T(8,128)} %slice.18), channel_id=1, source_target_pairs={{1,0},{2,1},{3,2},{4,3},{5,4},{6,5},{7,6},{0,7},{9,8},{10,9},{11,1... | collective-permute-start | bytes 3145736 | tf_op jit(solution)/shard_map/ppermute | solution.py:30
  10.7 13.7 %collective-permute-start.2 = (s32[1,16]{1,0:T(1,128)S(1)}, s32[1,16]{1,0:T(1,128)S(1)}, u32[]{:S(2)}, u32[]{:S(2)}) collective-permute-start(s32[1,16]{1,0:T(1,128)S(1)} %add_bitcast_fusion), channel_id=1, source_target_pairs={{1,0},{2,1},{3,2},{4,3},{5,4},{6,5},{7,6},{0,7},{9,8},{10,9},{11,1... | collective-permute-start | bytes 200 | tf_op jit(solution)/shard_map/ppermute | solution.py:30
  13.9 10.6 %collective-permute-start.1 = (s32[1,16]{1,0:T(1,128)S(1)}, s32[1,16]{1,0:T(1,128)S(1)}, u32[]{:S(2)}, u32[]{:S(2)}) collective-permute-start(s32[1,16]{1,0:T(1,128)S(1)} %add_bitcast_fusion), channel_id=1, source_target_pairs={{7,0},{0,1},{1,2},{2,3},{3,4},{4,5},{5,6},{6,7},{15,8},{8,9},{9,10... | collective-permute-start | bytes 200 | tf_op jit(solution)/shard_map/ppermute | solution.py:30
  24.5 5.3 %collective-permute-start.4 = (s32[3,16]{1,0:T(4,128)S(1)}, s32[3,16]{1,0:T(4,128)S(1)}, u32[]{:S(2)}, u32[]{:S(2)}) collective-permute-start(s32[3,16]{1,0:T(4,128)S(1)} %pad_add_fusion), channel_id=1, source_target_pairs={{8,0},{16,8},{24,16},{32,24},{40,32},{48,40},{56,48},{64,56},{72,6... | collective-permute-start | bytes 584 | tf_op jit(solution)/shard_map/ppermute | solution.py:30
  25.1 5.8 %collective-permute-start.3 = (s32[3,16]{1,0:T(4,128)S(1)}, s32[3,16]{1,0:T(4,128)S(1)}, u32[]{:S(2)}, u32[]{:S(2)}) collective-permute-start(s32[3,16]{1,0:T(4,128)S(1)} %pad_add_fusion), channel_id=1, source_target_pairs={{120,0},{0,8},{8,16},{16,24},{24,32},{32,40},{40,48},{48,56},{56,6... | collective-permute-start | bytes 584 | tf_op jit(solution)/shard_map/ppermute | solution.py:30
  31.0 3.7 %copy-start.8 = (f32[2,256,512]{2,1,0:T(8,128)}, f32[2,256,512]{2,1,0:T(8,128)S(1)}, u32[]{:S(2)}) copy-start(f32[2,256,512]{2,1,0:T(8,128)S(1)} %collective-permute-done.below) | copy-start | bytes 3145732
  31.9 9.2 %collective-permute-start.6 = (f32[2,256,256]{2,1,0:T(8,128)}, f32[2,256,256]{2,1,0:T(8,128)}, u32[]{:S(2)}, u32[]{:S(2)}) collective-permute-start(f32[2,256,256]{2,1,0:T(8,128)} %slice.19), channel_id=1, source_target_pairs={{1,0},{2,1},{3,2},{4,3},{5,4},{6,5},{7,6},{0,7},{9,8},{10,9},{11,1... | collective-permute-start | bytes 1572872 | tf_op jit(solution)/shard_map/ppermute | solution.py:30
  34.7 6.4 %copy-start.1 = (bf16[512,1536]{1,0:T(8,128)(2,1)S(1)}, bf16[512,1536]{1,0:T(8,128)(2,1)}, u32[]{:S(2)}) copy-start(bf16[512,1536]{1,0:T(8,128)(2,1)} %constant.20.clone.left) | copy-start | bytes 4718596
  35.7 5.4 %copy-start = (bf16[1536,512]{1,0:T(8,128)(2,1)S(1)}, bf16[1536,512]{1,0:T(8,128)(2,1)}, u32[]{:S(2)}) copy-start(bf16[1536,512]{1,0:T(8,128)(2,1)} %constant.21.clone.right) | copy-start | bytes 4718596
  36.5 1.0 copy-start.7
  41.1 1.2 copy-start.2
  42.3 1.6 copy-start.5
  43.9 1.2 copy-start.9
  57.3 33.2 %collective-permute-start.9 = (f32[2,768,256]{2,1,0:T(8,128)S(1)}, f32[2,768,256]{2,1,0:T(8,128)S(1)}, u32[]{:S(2)}, u32[]{:S(2)}) collective-permute-start(f32[2,768,256]{2,1,0:T(8,128)S(1)} %get-tuple-element.79.refs_2_.zl), channel_id=1, source_target_pairs={{1,0},{2,1},{3,2},{4,3},{5,4},{6,5},{7,6},{0,7},{9,8},{10,9},{11,1... | collective-permute-start | bytes 4718600 | tf_op jit(solution)/shard_map/ppermute | solution.py:30
  57.3 33.2 %collective-permute-start.7 = (f32[2,768,256]{2,1,0:T(8,128)S(1)}, f32[2,768,256]{2,1,0:T(8,128)S(1)}, u32[]{:S(2)}, u32[]{:S(2)}) collective-permute-start(f32[2,768,256]{2,1,0:T(8,128)S(1)} %get-tuple-element.81.refs_4_.zr), channel_id=1, source_target_pairs={{7,0},{0,1},{1,2},{2,3},{3,4},{4,5},{5,6},{6,7},{15,8},{8,9},{9,10... | collective-permute-start | bytes 4718600 | tf_op jit(solution)/shard_map/ppermute | solution.py:30
  59.1 31.4 %collective-permute-start.8 = (f32[3,256,256]{2,1,0:T(8,128)S(1)}, f32[3,256,256]{2,1,0:T(8,128)S(1)}, u32[]{:S(2)}, u32[]{:S(2)}) collective-permute-start(f32[3,256,256]{2,1,0:T(8,128)S(1)} %get-tuple-element.75.dn), channel_id=1, source_target_pairs={{120,0},{0,8},{8,16},{16,24},{24,32},{32,40},{40,48},{48,56},{56,6... | collective-permute-start | bytes 2359304 | tf_op jit(solution)/shard_map/ppermute | solution.py:30
  59.1 31.4 %collective-permute-start.10 = (f32[3,256,256]{2,1,0:T(8,128)S(1)}, f32[3,256,256]{2,1,0:T(8,128)S(1)}, u32[]{:S(2)}, u32[]{:S(2)}) collective-permute-start(f32[3,256,256]{2,1,0:T(8,128)S(1)} %get-tuple-element.76.up), channel_id=1, source_target_pairs={{8,0},{16,8},{24,16},{32,24},{40,32},{48,40},{56,48},{64,56},{72,6... | collective-permute-start | bytes 2359304 | tf_op jit(solution)/shard_map/ppermute | solution.py:30
  90.8 41.0 %copy-start.3 = (f32[1,1,4,256,256]{4,3,2,1,0:T(8,128)S(1)}, f32[1,1,4,256,256]{4,3,2,1,0:T(8,128)}, u32[]{:S(2)}) copy-start(f32[1,1,4,256,256]{4,3,2,1,0:T(8,128)} %param.9) | copy-start | bytes 3145732
  90.9 41.0 %collective-permute-start.11 = (f32[2,2,256,256]{3,2,1,0:T(8,128)S(1)}, f32[2,2,256,256]{3,2,1,0:T(8,128)S(1)}, u32[]{:S(2)}, u32[]{:S(2)}) collective-permute-start(f32[2,2,256,256]{3,2,1,0:T(8,128)S(1)} %get-tuple-element.83), channel_id=1, source_target_pairs={{8,0},{16,8},{24,16},{32,24},{40,32},{48,40},{56,48},{64,56},{72,6... | collective-permute-start | bytes 3145736 | tf_op jit(solution)/shard_map/ppermute | solution.py:30
  96.6 35.3 %collective-permute-start.12 = (f32[2,2,256,256]{3,2,1,0:T(8,128)S(1)}, f32[2,2,256,256]{3,2,1,0:T(8,128)S(1)}, u32[]{:S(2)}, u32[]{:S(2)}) collective-permute-start(f32[2,2,256,256]{3,2,1,0:T(8,128)S(1)} %get-tuple-element.84), channel_id=1, source_target_pairs={{120,0},{0,8},{8,16},{16,24},{24,32},{32,40},{40,48},{48,56},{56,6... | collective-permute-start | bytes 3145736 | tf_op jit(solution)/shard_map/ppermute | solution.py:30
  144.5 32.6 %collective-permute-start.15 = (f32[2,768,256]{2,1,0:T(8,128)S(1)}, f32[2,768,256]{2,1,0:T(8,128)S(1)}, u32[]{:S(2)}, u32[]{:S(2)}) collective-permute-start(f32[2,768,256]{2,1,0:T(8,128)S(1)} %get-tuple-element.100.refs_2_.zl), channel_id=1, source_target_pairs={{1,0},{2,1},{3,2},{4,3},{5,4},{6,5},{7,6},{0,7},{9,8},{10,9},{11,1... | collective-permute-start | bytes 4718600 | tf_op jit(solution)/shard_map/ppermute | solution.py:30
  144.6 32.6 %collective-permute-start.13 = (f32[2,768,256]{2,1,0:T(8,128)S(1)}, f32[2,768,256]{2,1,0:T(8,128)S(1)}, u32[]{:S(2)}, u32[]{:S(2)}) collective-permute-start(f32[2,768,256]{2,1,0:T(8,128)S(1)} %get-tuple-element.102.refs_4_.zr), channel_id=1, source_target_pairs={{7,0},{0,1},{1,2},{2,3},{3,4},{4,5},{5,6},{6,7},{15,8},{8,9},{9,10... | collective-permute-start | bytes 4718600 | tf_op jit(solution)/shard_map/ppermute | solution.py:30
  146.3 30.8 %collective-permute-start.14 = (f32[3,256,256]{2,1,0:T(8,128)S(1)}, f32[3,256,256]{2,1,0:T(8,128)S(1)}, u32[]{:S(2)}, u32[]{:S(2)}) collective-permute-start(f32[3,256,256]{2,1,0:T(8,128)S(1)} %get-tuple-element.96.dn), channel_id=1, source_target_pairs={{120,0},{0,8},{8,16},{16,24},{24,32},{32,40},{40,48},{48,56},{56,6... | collective-permute-start | bytes 2359304 | tf_op jit(solution)/shard_map/ppermute | solution.py:30
  146.3 30.8 %collective-permute-start.16 = (f32[3,256,256]{2,1,0:T(8,128)S(1)}, f32[3,256,256]{2,1,0:T(8,128)S(1)}, u32[]{:S(2)}, u32[]{:S(2)}) collective-permute-start(f32[3,256,256]{2,1,0:T(8,128)S(1)} %get-tuple-element.97.up), channel_id=1, source_target_pairs={{8,0},{16,8},{24,16},{32,24},{40,32},{48,40},{56,48},{64,56},{72,6... | collective-permute-start | bytes 2359304 | tf_op jit(solution)/shard_map/ppermute | solution.py:30
  177.5 44.8 %collective-permute-start.17 = (f32[2,2,256,256]{3,2,1,0:T(8,128)S(1)}, f32[2,2,256,256]{3,2,1,0:T(8,128)S(1)}, u32[]{:S(2)}, u32[]{:S(2)}) collective-permute-start(f32[2,2,256,256]{3,2,1,0:T(8,128)S(1)} %get-tuple-element.104), channel_id=1, source_target_pairs={{8,0},{16,8},{24,16},{32,24},{40,32},{48,40},{56,48},{64,56},{72,6... | collective-permute-start | bytes 3145736 | tf_op jit(solution)/shard_map/ppermute | solution.py:30
  181.4 40.9 %collective-permute-start.18 = (f32[2,2,256,256]{3,2,1,0:T(8,128)S(1)}, f32[2,2,256,256]{3,2,1,0:T(8,128)S(1)}, u32[]{:S(2)}, u32[]{:S(2)}) collective-permute-start(f32[2,2,256,256]{3,2,1,0:T(8,128)S(1)} %get-tuple-element.105), channel_id=1, source_target_pairs={{120,0},{0,8},{8,16},{16,24},{24,32},{32,40},{40,48},{48,56},{56,6... | collective-permute-start | bytes 3145736 | tf_op jit(solution)/shard_map/ppermute | solution.py:30
  235.0 31.7 %collective-permute-start.19 = (f32[2,768,256]{2,1,0:T(8,128)S(1)}, f32[2,768,256]{2,1,0:T(8,128)S(1)}, u32[]{:S(2)}, u32[]{:S(2)}) collective-permute-start(f32[2,768,256]{2,1,0:T(8,128)S(1)} %get-tuple-element.117), channel_id=1, source_target_pairs={{7,0},{0,1},{1,2},{2,3},{3,4},{4,5},{5,6},{6,7},{15,8},{8,9},{9,10... | collective-permute-start | bytes 4718600 | tf_op jit(solution)/shard_map/ppermute | solution.py:30
  235.0 31.7 %collective-permute-start.20 = (f32[3,256,256]{2,1,0:T(8,128)S(1)}, f32[3,256,256]{2,1,0:T(8,128)S(1)}, u32[]{:S(2)}, u32[]{:S(2)}) collective-permute-start(f32[3,256,256]{2,1,0:T(8,128)S(1)} %get-tuple-element.119), channel_id=1, source_target_pairs={{120,0},{0,8},{8,16},{16,24},{24,32},{32,40},{40,48},{48,56},{56,6... | collective-permute-start | bytes 2359304 | tf_op jit(solution)/shard_map/ppermute | solution.py:30
  267.4 27.9 %collective-permute-start.21 = (f32[1,2,256,256]{3,2,1,0:T(8,128)S(1)}, f32[1,2,256,256]{3,2,1,0:T(8,128)S(1)}, u32[]{:S(2)}, u32[]{:S(2)}) collective-permute-start(f32[1,2,256,256]{3,2,1,0:T(8,128)S(1)} %get-tuple-element.124), channel_id=1, source_target_pairs={{120,0},{0,8},{8,16},{16,24},{24,32},{32,40},{40,48},{48,56},{56,6... | collective-permute-start | bytes 1572872 | tf_op jit(solution)/shard_map/ppermute | solution.py:30
